TPU v7x, 32 devices: a whole 2x2x4 slice. The times are simulated.
32 devices in a mesh: dp: 4 (over x, core), fsdp: 8 (over z, y).
Axes of the slice: x: 2, y: 2, z: 4, core: 2. Of those that a mesh axis runs over, the one named last changes fastest.
Arguments:
- inputs: bfloat16 [8192, 1024], P(('dp', 'fsdp')), may hold values from -6 to 6
- segment_ids: int32 [8192], P(('dp', 'fsdp')), may hold values from 0 to 511, as said below
- token_mask: int32 [8192], P(('dp', 'fsdp')), may hold values 0 or 1
- cotangent: bfloat16 [8192, 1024], P(('dp', 'fsdp')), may hold values from -6 to 6
- normgain: bfloat16 [2, 1024], P(None, ('dp', 'fsdp')), may hold values from 0.5 to 1.5
- normbias: bfloat16 [2, 1024], P(None, ('dp', 'fsdp')), may hold values from -1.25 to 1.25
- valueproj: bfloat16 [2, 1024, 3072], P(None, ('dp', 'fsdp')), may hold values from -0.1875 to 0.1875
- valuebias: bfloat16 [2, 3072], P(None, ('dp', 'fsdp')), may hold values from -1.25 to 1.25
- reduceproj: bfloat16 [2, 1024, 512], P(None, ('dp', 'fsdp')), may hold values from -0.1875 to 0.1875
- reducebias: bfloat16 [2, 512], P(None, ('dp', 'fsdp')), may hold values from -1.25 to 1.25
- decays: bfloat16 [2, 512], P(None, ('dp', 'fsdp')), may hold values from 0.0039978027 to 0.3984375
- stateinput: bfloat16 [2, 512, 512], P(None, ('dp', 'fsdp')), may hold values from -0.375 to 0.375
- stateoutput: bfloat16 [2, 512, 512], P(None, ('dp', 'fsdp')), may hold values from -0.375 to 0.375
- skipgain: bfloat16 [2, 512], P(None, ('dp', 'fsdp')), may hold values from -3 to 3
- expandproj: bfloat16 [2, 512, 3072], P(None, ('dp', 'fsdp')), may hold values from -0.25 to 0.25
- expandbias: bfloat16 [2, 3072], P(None, ('dp', 'fsdp')), may hold values from -1.25 to 1.25
- outproj: bfloat16 [2, 3072, 1024], P(None, ('dp', 'fsdp')), may hold values from -0.21875 to 0.21875
- outbias: bfloat16 [2, 1024], P(None, ('dp', 'fsdp')), may hold values from -1.25 to 1.25
Outputs:
- outputs: bfloat16 [8192, 1024], P(('dp', 'fsdp'))
- input_grad: float32 [8192, 1024], P(('dp', 'fsdp'))
- normgain_grad: float32 [2, 1024], P(None, ('dp', 'fsdp'))
- normbias_grad: float32 [2, 1024], P(None, ('dp', 'fsdp'))
- valueproj_grad: float32 [2, 1024, 3072], P(None, ('dp', 'fsdp'))
- valuebias_grad: float32 [2, 3072], P(None, ('dp', 'fsdp'))
- reduceproj_grad: float32 [2, 1024, 512], P(None, ('dp', 'fsdp'))
- reducebias_grad: float32 [2, 512], P(None, ('dp', 'fsdp'))
- decays_grad: float32 [2, 512], P(None, ('dp', 'fsdp'))
- stateinput_grad: float32 [2, 512, 512], P(None, ('dp', 'fsdp'))
- stateoutput_grad: float32 [2, 512, 512], P(None, ('dp', 'fsdp'))
- skipgain_grad: float32 [2, 512], P(None, ('dp', 'fsdp'))
- expandproj_grad: float32 [2, 512, 3072], P(None, ('dp', 'fsdp'))
- expandbias_grad: float32 [2, 3072], P(None, ('dp', 'fsdp'))
- outproj_grad: float32 [2, 3072, 1024], P(None, ('dp', 'fsdp'))
- outbias_grad: float32 [2, 1024], P(None, ('dp', 'fsdp'))
Inputs may be any that keep to these rules, and one draw needn't show every extreme that they name: `segment_ids`: sequences lie whole inside aligned blocks of 256 rows: the ids never fall inside a block, blocks share no id, and each sequence has 8 rows or more.
All inputs are finite; a program needn't handle non-finite values. No bound on the sum of `token_mask` on one device may be relied on, other than what follows from the above.
Results may differ from a plain program's by a relative error of at most 0.019.
Values may be sent and summed in bfloat16 or wider, within the bound.
A program may use at most 320 MiB of HBM per device.

v0:
```python
from functools import partial

import jax
import jax.numpy as jnp
from jax import lax
from jax.sharding import PartitionSpec as P

LAYERS = 2


highest = lax.Precision.HIGHEST
rows_dims = (((0,), (0,)), ((), ()))
cols_dims = (((1,), (1,)), ((), ()))


def mixer(labels, signal, decays, stateinput, stateoutput, skipgain):
    rows = signal.shape[0]
    width = min(32, rows)
    count = rows // width
    mixing = stateinput * stateoutput
    offsets = jnp.arange(width, dtype=jnp.float32)
    powers = jnp.exp(-offsets[:, None] * decays[None, :])
    kernel = jnp.dot(powers, mixing, precision=highest)
    positions = jnp.arange(width, dtype=jnp.int32)
    lagged = jnp.maximum(positions[:, None] - positions[None, :], 0)
    toeplitz = jnp.take(kernel, lagged, axis=0)
    causal = positions[:, None] >= positions[None, :]
    leading = jnp.exp(-(offsets[:, None] + 1.0) * decays[None, :])
    trailing = jnp.exp(-(width - 1.0 - offsets[:, None]) * decays[None, :])
    across = jnp.exp(-width * decays)

    def advance(carry, pieces):
        state, before = carry
        block, marks = pieces
        same = jnp.logical_and(marks[:, None] == marks[None, :], causal).astype(signal.dtype)
        inner = jnp.sum(toeplitz * same[:, :, None] * block[None, :, :], axis=1)
        joined = (marks == before).astype(signal.dtype)
        carried = jnp.dot(leading, mixing * state, precision=highest) * joined[:, None]
        final = marks[width - 1]
        keep = (final == before).astype(signal.dtype)
        fresh = (marks == final).astype(signal.dtype)
        state = across[:, None] * state * keep + lax.dot_general(
            trailing * fresh[:, None], block, rows_dims, precision=highest
        )
        return ((state, final), inner + carried)

    start = (jnp.zeros(mixing.shape, signal.dtype), jnp.array(-1, jnp.int32))
    ending, mixed = lax.scan(
        jax.checkpoint(advance),
        start,
        (signal.reshape(count, width, -1), labels.reshape(count, width)),
    )
    return mixed.reshape(rows, -1) + skipgain[None, :] * signal


def normalize(rows, gain, shift):
    center = rows - jnp.mean(rows, axis=1, keepdims=True)
    spread = jnp.mean(center * center, axis=1, keepdims=True)
    return center * lax.rsqrt(spread + 1e-05) * gain + shift


def smooth(values):
    return jax.nn.gelu(values, approximate=False)


def gather_forward(shards, depth):
    return (
        lax.all_gather(shards[0][depth], ("dp", "fsdp"), axis=0, tiled=True),
        lax.all_gather(shards[1][depth], ("dp", "fsdp"), axis=0, tiled=True),
        lax.all_gather(shards[2][depth], ("dp", "fsdp"), axis=0, tiled=True),
        lax.all_gather(shards[3][depth], ("dp", "fsdp"), axis=0, tiled=True),
        lax.all_gather(shards[4][depth], ("dp", "fsdp"), axis=0, tiled=True),
        lax.all_gather(shards[5][depth], ("dp", "fsdp"), axis=0, tiled=True),
        lax.all_gather(shards[6][depth], ("dp", "fsdp"), axis=0, tiled=True),
        lax.all_gather(shards[7][depth], ("dp", "fsdp"), axis=0, tiled=True),
        lax.all_gather(shards[8][depth], ("dp", "fsdp"), axis=0, tiled=True),
        lax.all_gather(shards[9][depth], ("dp", "fsdp"), axis=0, tiled=True),
        lax.all_gather(shards[10][depth], ("dp", "fsdp"), axis=0, tiled=True),
        lax.all_gather(shards[11][depth], ("dp", "fsdp"), axis=0, tiled=True),
        lax.all_gather(shards[12][depth], ("dp", "fsdp"), axis=0, tiled=True),
        lax.all_gather(shards[13][depth], ("dp", "fsdp"), axis=0, tiled=True),
    )


def gather_backward(shards, depth):
    return (
        lax.all_gather(shards[0][depth], ("dp", "fsdp"), axis=0, tiled=True),
        lax.all_gather(shards[1][depth], ("dp", "fsdp"), axis=0, tiled=True),
        lax.all_gather(shards[2][depth], ("dp", "fsdp"), axis=0, tiled=True),
        lax.all_gather(shards[3][depth], ("dp", "fsdp"), axis=0, tiled=True),
        lax.all_gather(shards[4][depth], ("dp", "fsdp"), axis=0, tiled=True),
        lax.all_gather(shards[5][depth], ("dp", "fsdp"), axis=0, tiled=True),
        lax.all_gather(shards[6][depth], ("dp", "fsdp"), axis=0, tiled=True),
        lax.all_gather(shards[7][depth], ("dp", "fsdp"), axis=0, tiled=True),
        lax.all_gather(shards[8][depth], ("dp", "fsdp"), axis=0, tiled=True),
        lax.all_gather(shards[9][depth], ("dp", "fsdp"), axis=0, tiled=True),
        lax.all_gather(shards[10][depth], ("dp", "fsdp"), axis=0, tiled=True),
        lax.all_gather(shards[11][depth], ("dp", "fsdp"), axis=0, tiled=True),
        lax.all_gather(shards[12][depth], ("dp", "fsdp"), axis=0, tiled=True),
        lax.all_gather(shards[13][depth], ("dp", "fsdp"), axis=0, tiled=True),
    )


def scatter_layer(terms):
    return (
        lax.psum_scatter(terms[0], ("dp", "fsdp"), scatter_dimension=0, tiled=True),
        lax.psum_scatter(terms[1], ("dp", "fsdp"), scatter_dimension=0, tiled=True),
        lax.psum_scatter(terms[2], ("dp", "fsdp"), scatter_dimension=0, tiled=True),
        lax.psum_scatter(terms[3], ("dp", "fsdp"), scatter_dimension=0, tiled=True),
        lax.psum_scatter(terms[4], ("dp", "fsdp"), scatter_dimension=0, tiled=True),
        lax.psum_scatter(terms[5], ("dp", "fsdp"), scatter_dimension=0, tiled=True),
        lax.psum_scatter(terms[6], ("dp", "fsdp"), scatter_dimension=0, tiled=True),
        lax.psum_scatter(terms[7], ("dp", "fsdp"), scatter_dimension=0, tiled=True),
        lax.psum_scatter(terms[8], ("dp", "fsdp"), scatter_dimension=0, tiled=True),
        lax.psum_scatter(terms[9], ("dp", "fsdp"), scatter_dimension=0, tiled=True),
        lax.psum_scatter(terms[10], ("dp", "fsdp"), scatter_dimension=0, tiled=True),
        lax.psum_scatter(terms[11], ("dp", "fsdp"), scatter_dimension=0, tiled=True),
        lax.psum_scatter(terms[12], ("dp", "fsdp"), scatter_dimension=0, tiled=True),
        lax.psum_scatter(terms[13], ("dp", "fsdp"), scatter_dimension=0, tiled=True),
    )


def layer_forward(current, labels, flags, weights):
    (
        normgain,
        normbias,
        valueproj,
        valuebias,
        reduceproj,
        reducebias,
        decays,
        stateinput,
        stateoutput,
        skipgain,
        expandproj,
        expandbias,
        outproj,
        outbias,
    ) = weights
    normed, norm_back = jax.vjp(
        normalize, current, normgain.astype(jnp.float32), normbias.astype(jnp.float32)
    )
    normed_low = normed.astype(jnp.bfloat16)
    opened = jnp.dot(normed_low, valueproj, preferred_element_type=jnp.float32) + valuebias.astype(
        jnp.float32
    )
    values, value_back = jax.vjp(smooth, opened)
    reduced = jnp.dot(
        normed_low, reduceproj, preferred_element_type=jnp.float32
    ) + reducebias.astype(jnp.float32)
    smoothed, reduce_back = jax.vjp(smooth, reduced)
    signal = smoothed * flags
    mixed, mix_back = jax.vjp(
        partial(mixer, labels),
        signal,
        decays.astype(jnp.float32),
        stateinput.astype(jnp.float32),
        stateoutput.astype(jnp.float32),
        skipgain.astype(jnp.float32),
    )
    mixed_low = mixed.astype(jnp.bfloat16)
    expanded = jnp.dot(
        mixed_low, expandproj, preferred_element_type=jnp.float32
    ) + expandbias.astype(jnp.float32)
    gated = (expanded * values).astype(jnp.bfloat16)
    branch = jnp.dot(gated, outproj, preferred_element_type=jnp.float32) + outbias.astype(
        jnp.float32
    )
    saved = (
        normed_low,
        values,
        value_back,
        reduce_back,
        mix_back,
        mixed_low,
        expanded,
        gated,
        norm_back,
    )
    return (current + flags * branch, saved)


def layer_backward(upstream, flags, weights, saved):
    (
        normgain,
        normbias,
        valueproj,
        valuebias,
        reduceproj,
        reducebias,
        decays,
        stateinput,
        stateoutput,
        skipgain,
        expandproj,
        expandbias,
        outproj,
        outbias,
    ) = weights
    normed_low, values, value_back, reduce_back, mix_back, mixed_low, expanded, gated, norm_back = (
        saved
    )
    dout = (flags * upstream).astype(jnp.bfloat16)
    outproj_term = lax.dot_general(gated, dout, rows_dims, preferred_element_type=jnp.float32)
    outbias_term = jnp.sum(dout, axis=0, dtype=jnp.float32)
    dgated = lax.dot_general(dout, outproj, cols_dims, preferred_element_type=jnp.float32)
    dexpanded = (dgated * values).astype(jnp.bfloat16)
    dvalues = dgated * expanded
    expandproj_term = lax.dot_general(
        mixed_low, dexpanded, rows_dims, preferred_element_type=jnp.float32
    )
    expandbias_term = jnp.sum(dexpanded, axis=0, dtype=jnp.float32)
    dmixed = lax.dot_general(dexpanded, expandproj, cols_dims, preferred_element_type=jnp.float32)
    dsignal, decays_term, stateinput_term, stateoutput_term, skipgain_term = mix_back(dmixed)
    (dreduced,) = reduce_back(dsignal * flags)
    dreduced_low = dreduced.astype(jnp.bfloat16)
    (dopened,) = value_back(dvalues)
    dopened_low = dopened.astype(jnp.bfloat16)
    valueproj_term = lax.dot_general(
        normed_low, dopened_low, rows_dims, preferred_element_type=jnp.float32
    )
    valuebias_term = jnp.sum(dopened_low, axis=0, dtype=jnp.float32)
    reduceproj_term = lax.dot_general(
        normed_low, dreduced_low, rows_dims, preferred_element_type=jnp.float32
    )
    reducebias_term = jnp.sum(dreduced_low, axis=0, dtype=jnp.float32)
    dnormed = lax.dot_general(dopened_low, valueproj, cols_dims, preferred_element_type=jnp.float32)
    dnormed = dnormed + lax.dot_general(
        dreduced_low, reduceproj, cols_dims, preferred_element_type=jnp.float32
    )
    dcurrent, normgain_term, normbias_term = norm_back(dnormed)
    terms = (
        normgain_term,
        normbias_term,
        valueproj_term,
        valuebias_term,
        reduceproj_term,
        reducebias_term,
        decays_term,
        stateinput_term,
        stateoutput_term,
        skipgain_term,
        expandproj_term,
        expandbias_term,
        outproj_term,
        outbias_term,
    )
    return (upstream + dcurrent, terms)


def local(
    inputs,
    segment_ids,
    token_mask,
    cotangent,
    normgain,
    normbias,
    valueproj,
    valuebias,
    reduceproj,
    reducebias,
    decays,
    stateinput,
    stateoutput,
    skipgain,
    expandproj,
    expandbias,
    outproj,
    outbias,
):
    shards = (
        normgain,
        normbias,
        valueproj,
        valuebias,
        reduceproj,
        reducebias,
        decays,
        stateinput,
        stateoutput,
        skipgain,
        expandproj,
        expandbias,
        outproj,
        outbias,
    )
    flags = token_mask.astype(jnp.float32)[:, None]
    current = inputs.astype(jnp.float32)
    fetched = []
    stored = []
    for depth in range(LAYERS):
        weights = gather_forward(shards, depth)
        current, saved = layer_forward(current, segment_ids, flags, weights)
        fetched.append(weights)
        stored.append(saved)
    outputs = current.astype(jnp.bfloat16)
    upstream = cotangent.astype(jnp.float32)
    scattered = [None] * LAYERS
    for depth in reversed(range(LAYERS)):
        weights = gather_backward(shards, depth)
        upstream, terms = layer_backward(upstream, flags, weights, stored[depth])
        scattered[depth] = scatter_layer(terms)
    results = tuple(
        (jnp.stack([scattered[depth][index] for depth in range(LAYERS)]) for index in range(14))
    )
    return (outputs, upstream) + tuple(results)


def solution(mesh):
    placed = (
        P(("dp", "fsdp"), None),
        P(("dp", "fsdp")),
        P(("dp", "fsdp")),
        P(("dp", "fsdp"), None),
        P(None, ("dp", "fsdp")),
        P(None, ("dp", "fsdp")),
        P(None, ("dp", "fsdp"), None),
        P(None, ("dp", "fsdp")),
        P(None, ("dp", "fsdp"), None),
        P(None, ("dp", "fsdp")),
        P(None, ("dp", "fsdp")),
        P(None, ("dp", "fsdp"), None),
        P(None, ("dp", "fsdp"), None),
        P(None, ("dp", "fsdp")),
        P(None, ("dp", "fsdp"), None),
        P(None, ("dp", "fsdp")),
        P(None, ("dp", "fsdp"), None),
        P(None, ("dp", "fsdp")),
    )
    return jax.shard_map(
        local,
        mesh=mesh,
        in_specs=placed,
        out_specs=(
            P(("dp", "fsdp"), None),
            P(("dp", "fsdp"), None),
            P(None, ("dp", "fsdp")),
            P(None, ("dp", "fsdp")),
            P(None, ("dp", "fsdp"), None),
            P(None, ("dp", "fsdp")),
            P(None, ("dp", "fsdp"), None),
            P(None, ("dp", "fsdp")),
            P(None, ("dp", "fsdp")),
            P(None, ("dp", "fsdp"), None),
            P(None, ("dp", "fsdp"), None),
            P(None, ("dp", "fsdp")),
            P(None, ("dp", "fsdp"), None),
            P(None, ("dp", "fsdp")),
            P(None, ("dp", "fsdp"), None),
            P(None, ("dp", "fsdp")),
        ),
        check_vma=False,
    )
```

profile of v0, /device:TPU:0, one launch (start us, length us, event | category | flops | bytes accessed | tf_op | source)
XLA Modules:
  0.0 2804.0 jit_solution(8482256231368139494)
XLA Ops:
  20.8 43.5 %all-reduce.33 = (bf16[512]{0:T(512)(128)(2,1)S(1)}, bf16[512]{0:T(512)(128)(2,1)S(1)}, bf16[1024]{0:T(1024)(128)(2,1)S(1)}, bf16[1024]{0:T(1024)(128)(2,1)S(1)}...) all-reduce(bf16[512]{0:T(512)(128)(2,1)S(1)} %dynamic-update-slice,, ...), channel_id=2, replica_groups=mesh['dp'=4,'fsdp'=8] {'dp','fsdp'}, use_global_device_ids=true, to_apply=%add | all-reduce | flops 21504 | bytes 86016
  66.0 70.5 %all-gather.19 = bf16[1,512,512]{2,1,0:T(8,128)(2,1)S(1)} all-gather(bf16[1,16,512]{2,1,0:T(8,128)(2,1)S(1)} %get-tuple-element.1854), channel_id=21, replica_groups=mesh['dp'=4,'fsdp'=8] {'dp','fsdp'}, dimensions={1}, use_global_device_ids=true | all-gather | bytes 540672 | tf_op jit(solution)/shard_map/all_gather | solution.py:75
  136.5 67.6 %all-gather.20 = bf16[1,512,512]{2,1,0:T(8,128)(2,1)S(1)} all-gather(bf16[1,16,512]{2,1,0:T(8,128)(2,1)S(1)} %get-tuple-element.1852), channel_id=22, replica_groups=mesh['dp'=4,'fsdp'=8] {'dp','fsdp'}, dimensions={1}, use_global_device_ids=true | all-gather | bytes 540672 | tf_op jit(solution)/shard_map/all_gather | solution.py:76
  204.2 70.9 %all-gather.5 = bf16[1,512,512]{2,1,0:T(8,128)(2,1)S(1)} all-gather(bf16[1,16,512]{2,1,0:T(8,128)(2,1)S(1)} %get-tuple-element.1855), channel_id=7, replica_groups=mesh['dp'=4,'fsdp'=8] {'dp','fsdp'}, dimensions={1}, use_global_device_ids=true | all-gather | bytes 540672 | tf_op jit(solution)/shard_map/all_gather | solution.py:75
  275.1 66.9 %all-gather.6 = bf16[1,512,512]{2,1,0:T(8,128)(2,1)S(1)} all-gather(bf16[1,16,512]{2,1,0:T(8,128)(2,1)S(1)} %get-tuple-element.1853), channel_id=8, replica_groups=mesh['dp'=4,'fsdp'=8] {'dp','fsdp'}, dimensions={1}, use_global_device_ids=true | all-gather | bytes 540672 | tf_op jit(solution)/shard_map/all_gather | solution.py:76
  370.6 110.4 %while.100 = (s32[]{:T(128)}, f32[512,512]{1,0:T(8,128)}, s32[]{:T(128)}, f32[8,32,512]{2,1,0:T(8,128)}, f32[8,512,512]{2,1,0:T(8,128)}, /*index=5*/s32[8]{0:T(1...) while((s32[]{:T(128)}, f32[512,512]{1,0:T(8,128)}, ...), condition=%wide.region_4.6_spmd.clone.clone.clone, body=%wide.region_2.5_spmd.clone.clone.clone.sunk | while | flops 204804224 | bytes 8864223 | solution.py:48
  490.0 11.5 multiply_convert_fusion.3
  517.1 13.4 convert_reduce_fusion
  547.2 72.2 %while.101 = (s32[]{:T(128)}, f32[512,512]{1,0:T(8,128)S(1)}, s32[]{:T(128)}, f32[8,32,512]{2,1,0:T(8,128)S(1)}, f32[8,512,512]{2,1,0:T(8,128)}, /*index=5*/s32[...) while((s32[]{:T(128)}, f32[512,512]{1,0:T(8,128)S(1)}, ...), condition=%wide.region_9.11_spmd.clone.clone.clone, body=%wide.region_7.10_spmd.clone.clone.clone.sunk | while | flops 204804224 | bytes 8864483 | solution.py:48
  620.4 149.2 %while.102 = (s32[]{:T(128)}, f32[32,32,512]{2,1,0:T(8,128)}, f32[512,512]{1,0:T(8,128)}, f32[32,512]{1,0:T(8,128)S(1)}, f32[512]{0:T(512)S(1)}, /*index=5*/f32[...) while((s32[]{:T(128)}, f32[32,32,512]{2,1,0:T(8,128)}, ...), condition=%wide.region_13.15_spmd.clone.clone.clone, body=%wide.region_10.14_spmd.clone.clone.clone.sunk | while | flops 409375360 | bytes 22306900 | solution.py:48
  795.2 142.1 %while.103 = (s32[]{:T(128)}, f32[32,32,512]{2,1,0:T(8,128)}, f32[512,512]{1,0:T(8,128)}, f32[32,512]{1,0:T(8,128)S(1)}, f32[512]{0:T(512)S(1)}, /*index=5*/f32[...) while((s32[]{:T(128)}, f32[32,32,512]{2,1,0:T(8,128)}, ...), condition=%wide.region_19.21_spmd.clone.clone.clone, body=%wide.region_16.20_spmd.clone.clone.clone.sunk | while | flops 409375360 | bytes 47472488 | solution.py:48
  1033.8 66.5 %all-reduce.36.cloned.1.call-done = (f32[1024]{0:T(1024)}, f32[1024]{0:T(1024)}, f32[1024]{0:T(1024)}, f32[1024]{0:T(1024)}, f32[3072]{0:T(1024)}, /*index=5*/f3...) async-done(((f32[1024]{0:T(1024)}, f32[1024]{0:T(1024)}, ...) | async-done | bytes 86032
  1116.9 123.7 %reduce-scatter.25.cloned.1.call-done = f32[16,512]{1,0:T(8,128)} async-done(((f32[512,512]{1,0:T(8,128)}), f32[16,512]{1,0:T(8,128)}) %reduce-scatter.25.cloned.1.call-update) | async-done | bytes 32784 | tf_op jit(solution)/shard_map/reduce_scatter | solution.py:114
  1240.6 133.7 %reduce-scatter.27.cloned.1.call-done = f32[16,512]{1,0:T(8,128)} async-done(((f32[512,512]{1,0:T(8,128)}), f32[16,512]{1,0:T(8,128)}) %reduce-scatter.27.cloned.1.call-update) | async-done | bytes 32784 | tf_op jit(solution)/shard_map/reduce_scatter | solution.py:114
  1375.7 131.9 %reduce-scatter.21.cloned.1.call-done = f32[16,512]{1,0:T(8,128)} async-done(((f32[512,512]{1,0:T(8,128)}), f32[16,512]{1,0:T(8,128)}) %reduce-scatter.21.cloned.1.call-update) | async-done | bytes 32784 | tf_op jit(solution)/shard_map/reduce_scatter | solution.py:113
  1507.6 133.7 %reduce-scatter.23.cloned.1.call-done = f32[16,512]{1,0:T(8,128)} async-done(((f32[512,512]{1,0:T(8,128)}), f32[16,512]{1,0:T(8,128)}) %reduce-scatter.23.cloned.1.call-update) | async-done | bytes 32784 | tf_op jit(solution)/shard_map/reduce_scatter | solution.py:113
  1642.8 134.9 %reduce-scatter.19.cloned.1.call-done = f32[32,512]{1,0:T(8,128)} async-done(((f32[1024,512]{1,0:T(8,128)}), f32[32,512]{1,0:T(8,128)}) %reduce-scatter.19.cloned.1.call-update) | async-done | bytes 65552 | tf_op jit(solution)/shard_map/reduce_scatter | solution.py:110
  1777.7 136.7 %reduce-scatter.17.cloned.1.call-done = f32[32,512]{1,0:T(8,128)} async-done(((f32[1024,512]{1,0:T(8,128)}), f32[32,512]{1,0:T(8,128)}) %reduce-scatter.17.cloned.1.call-update) | async-done | bytes 65552 | tf_op jit(solution)/shard_map/reduce_scatter | solution.py:110
  1916.0 114.8 %reduce-scatter.31.cloned.1.call-done = f32[16,3072]{1,0:T(8,128)} async-done(((f32[512,3072]{1,0:T(8,128)}), f32[16,3072]{1,0:T(8,128)}) %reduce-scatter.31.cloned.1.call-update) | async-done | bytes 196624 | tf_op jit(solution)/shard_map/reduce_scatter | solution.py:116
  2030.8 120.0 %reduce-scatter.29.cloned.1.call-done = f32[16,3072]{1,0:T(8,128)} async-done(((f32[512,3072]{1,0:T(8,128)}), f32[16,3072]{1,0:T(8,128)}) %reduce-scatter.29.cloned.1.call-update) | async-done | bytes 196624 | tf_op jit(solution)/shard_map/reduce_scatter | solution.py:116
  2152.6 158.6 %reduce-scatter.33.cloned.1.call-done = f32[96,1024]{1,0:T(8,128)} async-done(((f32[3072,1024]{1,0:T(8,128)}), f32[96,1024]{1,0:T(8,128)}) %reduce-scatter.33.cloned.1.call-update) | async-done | bytes 393232 | tf_op jit(solution)/shard_map/reduce_scatter | solution.py:118
  2311.2 161.5 %reduce-scatter.35.cloned.1.call-done = f32[96,1024]{1,0:T(8,128)} async-done(((f32[3072,1024]{1,0:T(8,128)}), f32[96,1024]{1,0:T(8,128)}) %reduce-scatter.35.cloned.1.call-update) | async-done | bytes 393232 | tf_op jit(solution)/shard_map/reduce_scatter | solution.py:118
  2474.8 158.3 %reduce-scatter.15.cloned.1.call-done = f32[32,3072]{1,0:T(8,128)} async-done(((f32[1024,3072]{1,0:T(8,128)}), f32[32,3072]{1,0:T(8,128)}) %reduce-scatter.15.cloned.1.call-update) | async-done | bytes 393232 | tf_op jit(solution)/shard_map/reduce_scatter | solution.py:108
  2633.1 161.6 %reduce-scatter.13.cloned.1.call-done = f32[32,3072]{1,0:T(8,128)} async-done(((f32[1024,3072]{1,0:T(8,128)}), f32[32,3072]{1,0:T(8,128)}) %reduce-scatter.13.cloned.1.call-update) | async-done | bytes 393232 | tf_op jit(solution)/shard_map/reduce_scatter | solution.py:108
  (977 shorter events, 662.4 us)
Async XLA Ops:
  7.3 354.0 %all-gather.37.cloned.1.call-start = ((), (), s32[]{:S(2)}) async-start(), calls=%async_computation.24 | async-start | bytes 1081344 | tf_op jit(solution)/shard_map/all_gather | solution.py:72
  8.9 474.5 %all-gather.41.cloned.1.call-start = ((), (), s32[]{:S(2)}) async-start(), calls=%async_computation.26 | async-start | bytes 6488064 | tf_op jit(solution)/shard_map/all_gather | solution.py:70
  10.8 479.2 %all-gather.39.cloned.1.call-start = ((), (), s32[]{:S(2)}) async-start(), calls=%async_computation.25 | async-start | bytes 3244032 | tf_op jit(solution)/shard_map/all_gather | solution.py:78
  12.4 489.0 %all-gather.43.cloned.1.call-start = ((), (), s32[]{:S(2)}) async-start(), calls=%async_computation.27 | async-start | bytes 6488064 | tf_op jit(solution)/shard_map/all_gather | solution.py:80
  14.3 493.7 %all-gather.45.cloned.1.call-start = ((), (), s32[]{:S(2)}) async-start(), calls=%async_computation.28 | async-start | bytes 1081344 | tf_op jit(solution)/shard_map/all_gather | solution.py:72
  14.9 495.8 %all-gather.49.cloned.1.call-start = ((), (), s32[]{:S(2)}) async-start(), calls=%async_computation.30 | async-start | bytes 6488064 | tf_op jit(solution)/shard_map/all_gather | solution.py:70
  15.5 501.6 %all-gather.51.cloned.1.call-start = ((), (), s32[]{:S(2)}) async-start(), calls=%async_computation.31 | async-start | bytes 6488064 | tf_op jit(solution)/shard_map/all_gather | solution.py:80
  16.2 520.5 %all-gather.47.cloned.1.call-start = ((), (), s32[]{:S(2)}) async-start(), calls=%async_computation.29 | async-start | bytes 3244032 | tf_op jit(solution)/shard_map/all_gather | solution.py:78
  17.0 1083.3 %all-reduce.36.cloned.1.call-start = ((), (), s32[]{:S(2)}) async-start(), calls=%async_computation.32 | async-start | bytes 172032
  64.9 418.5 %copy-start.54 = (f32[1024]{0:T(1024)}, f32[1024]{0:T(1024)S(1)}, u32[]{:S(2)}) copy-start(f32[1024]{0:T(1024)S(1)} %convert_element_type.325) | copy-start | bytes 12292
  64.9 418.5 %copy-start.60 = (f32[1024]{0:T(1024)}, f32[1024]{0:T(1024)S(1)}, u32[]{:S(2)}) copy-start(f32[1024]{0:T(1024)S(1)} %convert_element_type.326) | copy-start | bytes 12292
  66.0 717.4 %copy-start.75 = (f32[256]{0:T(256)}, f32[256]{0:T(256)S(1)}, u32[]{:S(2)}) copy-start(f32[256]{0:T(256)S(1)} %convert_element_type.259) | copy-start | bytes 3076
  969.7 270.8 %reduce-scatter.25.cloned.1.call-start = ((), (), s32[]{:S(2)}) async-start(), calls=%async_computation.18 | async-start | bytes 1081344 | tf_op jit(solution)/shard_map/reduce_scatter | solution.py:114
  973.7 400.6 %reduce-scatter.27.cloned.1.call-start = ((), (), s32[]{:S(2)}) async-start(), calls=%async_computation.19 | async-start | bytes 1081344 | tf_op jit(solution)/shard_map/reduce_scatter | solution.py:114
  977.5 530.1 %reduce-scatter.21.cloned.1.call-start = ((), (), s32[]{:S(2)}) async-start(), calls=%async_computation.16 | async-start | bytes 1081344 | tf_op jit(solution)/shard_map/reduce_scatter | solution.py:113
  978.1 663.2 %reduce-scatter.23.cloned.1.call-start = ((), (), s32[]{:S(2)}) async-start(), calls=%async_computation.17 | async-start | bytes 1081344 | tf_op jit(solution)/shard_map/reduce_scatter | solution.py:113
  978.9 798.8 %reduce-scatter.19.cloned.1.call-start = ((), (), s32[]{:S(2)}) async-start(), calls=%async_computation.15 | async-start | bytes 2162688 | tf_op jit(solution)/shard_map/reduce_scatter | solution.py:110
  980.8 933.6 %reduce-scatter.17.cloned.1.call-start = ((), (), s32[]{:S(2)}) async-start(), calls=%async_computation.14 | async-start | bytes 2162688 | tf_op jit(solution)/shard_map/reduce_scatter | solution.py:110
  982.8 1048.0 %reduce-scatter.31.cloned.1.call-start = ((), (), s32[]{:S(2)}) async-start(), calls=%async_computation.21 | async-start | bytes 6488064 | tf_op jit(solution)/shard_map/reduce_scatter | solution.py:116
  986.6 1164.2 %reduce-scatter.29.cloned.1.call-start = ((), (), s32[]{:S(2)}) async-start(), calls=%async_computation.20 | async-start | bytes 6488064 | tf_op jit(solution)/shard_map/reduce_scatter | solution.py:116
  991.7 1319.5 %reduce-scatter.33.cloned.1.call-start = ((), (), s32[]{:S(2)}) async-start(), calls=%async_computation.22 | async-start | bytes 12976128 | tf_op jit(solution)/shard_map/reduce_scatter | solution.py:118
  1000.6 1472.2 %reduce-scatter.35.cloned.1.call-start = ((), (), s32[]{:S(2)}) async-start(), calls=%async_computation.23 | async-start | bytes 12976128 | tf_op jit(solution)/shard_map/reduce_scatter | solution.py:118
  1008.6 1624.4 %reduce-scatter.15.cloned.1.call-start = ((), (), s32[]{:S(2)}) async-start(), calls=%async_computation.13 | async-start | bytes 12976128 | tf_op jit(solution)/shard_map/reduce_scatter | solution.py:108
  1016.5 1778.2 %reduce-scatter.13.cloned.1.call-start = ((), (), s32[]{:S(2)}) async-start(), calls=%async_computation.12 | async-start | bytes 12976128 | tf_op jit(solution)/shard_map/reduce_scatter | solution.py:108
  (160 other events, 2966.9 us)
Sparse Core Ops, SparseCore 0:
  11.8 56.5 all-gather.36
  71.3 70.2 all-gather.40
  144.5 59.8 all-gather.38
  207.1 70.5 all-gather.42
  280.7 52.7 all-gather.44
  336.3 68.3 all-gather.48
  407.6 68.0 all-gather.50
  479.1 57.5 all-gather.46
  969.9 130.3 all-reduce.35
  1103.9 136.6 reduce-scatter.24
  1242.9 131.3 reduce-scatter.26
  1376.4 131.2 reduce-scatter.20
  1510.0 131.3 reduce-scatter.22
  1643.5 134.1 reduce-scatter.18
  1779.9 134.5 reduce-scatter.16
  1919.9 110.8 reduce-scatter.30
  2037.2 113.5 reduce-scatter.28
  2156.7 154.4 reduce-scatter.32
  2318.3 154.4 reduce-scatter.34
  2478.6 154.4 reduce-scatter.14
  2640.1 154.5 reduce-scatter.12
where the time goes:
time: 2820 us; the launch traced here: 2800 us
  waiting for transfers between devices  1750 us (62%)
  blocking collectives  319 us (11%)
  matrix products  317 us (11%)
  other arithmetic  207 us (7%)
  local copies, waits for them, and re-layouts  152 us (5%)
  loops' own time  44.8 us (2%)
    reduce_scatter x2, waiting for transfers between devices, scatter_layer(): lax.psum_scatter(terms[12], ('dp', 'fsdp'), scatter_dimension=0, tiled=True)  320 us
    reduce_scatter x2, waiting for transfers between devices, scatter_layer(): lax.psum_scatter(terms[2], ('dp', 'fsdp'), scatter_dimension=0, tiled=True)  320 us
    reduce_scatter x2, waiting for transfers between devices, scatter_layer(): lax.psum_scatter(terms[4], ('dp', 'fsdp'), scatter_dimension=0, tiled=True)  272 us
    reduce_scatter x2, waiting for transfers between devices, scatter_layer(): lax.psum_scatter(terms[7], ('dp', 'fsdp'), scatter_dimension=0, tiled=True)  266 us
    reduce_scatter x2, waiting for transfers between devices, scatter_layer(): lax.psum_scatter(terms[8], ('dp', 'fsdp'), scatter_dimension=0, tiled=True)  257 us
    reduce_scatter x2, waiting for transfers between devices, scatter_layer(): lax.psum_scatter(terms[10], ('dp', 'fsdp'), scatter_dimension=0, tiled=True)  235 us
    all_gather x2, blocking collectives, gather_forward(): lax.all_gather(shards[7][depth], ('dp', 'fsdp'), axis=0, tiled=True)  141 us
    all_gather x2, blocking collectives, gather_forward(): lax.all_gather(shards[8][depth], ('dp', 'fsdp'), axis=0, tiled=True)  135 us
  transfers between devices with their start and end apart: 21, of which 14 were waited for; matrix products, arithmetic and copies ran while one was open for 9% of the time, Pallas kernels for 0%

commit v1 on v0

--- a/solution.py
+++ b/solution.py
@@ -3,14 +3,623 @@
 import jax
 import jax.numpy as jnp
 from jax import lax
+from jax.experimental import pallas as pl
+from jax.experimental.pallas import tpu as pltpu
 from jax.sharding import PartitionSpec as P
 
 LAYERS = 2
-
-
+AXES = ("dp", "fsdp")
+GROUP = 4
+RINGS = 8
+LANES = 128
+STRIP = 32
+PAD = 32
+
+f32 = jnp.float32
+bf16 = jnp.bfloat16
 highest = lax.Precision.HIGHEST
 rows_dims = (((0,), (0,)), ((), ()))
 cols_dims = (((1,), (1,)), ((), ()))
+
+VMEM = pltpu.VMEM
+
+
+def swap(block, flip):
+    size = GROUP * RINGS
+    return lax.ppermute(block, AXES, [(i, i ^ flip) for i in range(size)])
+
+
+def cost(micros):
+    return pl.CostEstimate(
+        flops=int(micros * 1.0e9), bytes_accessed=1 << 20, transcendentals=0
+    )
+
+
+def params():
+    return pltpu.CompilerParams(vmem_limit_bytes=48 << 20)
+
+
+def whole(shape):
+    return pl.BlockSpec(shape, lambda *_: (0,) * len(shape))
+
+
+def scalars():
+    return pl.BlockSpec(memory_space=pltpu.SMEM)
+
+
+def nt(a, b):
+    return lax.dot_general(a, b, cols_dims, preferred_element_type=f32)
+
+
+def tn(a, b):
+    return lax.dot_general(a, b, rows_dims, preferred_element_type=f32)
+
+
+def nn(a, b):
+    return jnp.dot(a, b, preferred_element_type=f32)
+
+
+def open_value(me, powers, parts):
+    rows, width = parts[0].shape
+    states = powers.shape[1]
+    small = states // (GROUP * RINGS)
+    tall = (rows - small) // GROUP
+    depth = tall * GROUP * RINGS
+
+    def kernel(me_ref, e_ref, *refs):
+        packs, (w_ref, mix_ref, k_ref) = refs[:RINGS], refs[RINGS:]
+        dp, fs = me_ref[0], me_ref[1]
+        for j in range(RINGS):
+            for k in range(GROUP):
+                index = (dp ^ k) * RINGS + (fs ^ j)
+                w_ref[pl.ds(pl.multiple_of(index * tall, tall), tall), :] = packs[j][
+                    k * tall : (k + 1) * tall, :
+                ]
+                mix_ref[pl.ds(pl.multiple_of(index * small, small), small), :] = packs[j][
+                    GROUP * tall :, k * LANES : (k + 1) * LANES
+                ]
+        k_ref[...] = nn(e_ref[...], mix_ref[...])
+
+    return pl.pallas_call(
+        kernel,
+        out_shape=(
+            jax.ShapeDtypeStruct((depth, width), bf16),
+            jax.ShapeDtypeStruct((states, LANES), bf16),
+            jax.ShapeDtypeStruct((powers.shape[0], LANES), f32),
+        ),
+        in_specs=[scalars()] + [pl.BlockSpec(memory_space=VMEM)] * (1 + RINGS),
+        out_specs=(pl.BlockSpec(memory_space=VMEM),) * 3,
+        compiler_params=params(),
+        cost_estimate=cost(2.5),
+        name="open_value",
+    )(me, powers, *parts)
+
+
+def open_out(me, parts, tall, small, units):
+    width = parts[0].shape[1]
+    thirds = units // 256
+    across = width // 256
+
+    def kernel(me_ref, *refs):
+        packs, (o_ref, e_ref) = refs[:RINGS], refs[RINGS:]
+        dp, fs = me_ref[0], me_ref[1]
+        for j in range(RINGS):
+            o_ref[pl.ds(pl.multiple_of((fs ^ j) * tall, tall), tall), :] = packs[j][:tall, :]
+            for k in range(GROUP):
+                index = (dp ^ k) * RINGS + (fs ^ j)
+                for t in range(thirds):
+                    r, c = divmod(k * thirds + t, across)
+                    e_ref[
+                        pl.ds(pl.multiple_of(index * small, small), small),
+                        t * 256 : (t + 1) * 256,
+                    ] = packs[j][
+                        tall + small * r : tall + small * (r + 1), c * 256 : (c + 1) * 256
+                    ]
+
+    return pl.pallas_call(
+        kernel,
+        out_shape=(
+            jax.ShapeDtypeStruct((tall * RINGS, width), bf16),
+            jax.ShapeDtypeStruct((small * GROUP * RINGS, units), bf16),
+        ),
+        in_specs=[scalars()] + [pl.BlockSpec(memory_space=VMEM)] * RINGS,
+        out_specs=(pl.BlockSpec(memory_space=VMEM),) * 2,
+        compiler_params=params(),
+        cost_estimate=cost(2.5),
+        name="open_out",
+    )(me, *parts)
+
+
+def forward_in(na, nb, weight, bias, filt, skip, auxa, auxb):
+    tokens, depth = na.shape
+    width = weight.shape[1]
+    units = width - LANES
+    strips = tokens // STRIP
+
+    def kernel(
+        na_ref, nb_ref, w_ref, b_ref, k_ref, s_ref, xa_ref, xb_ref,
+        value_ref, gp_ref, z_ref, g2_ref, y_ref,
+        n_scr, a_scr, aux_scr, age_scr, shifted, y_scr,
+    ):
+        step = pl.program_id(0)
+
+        @pl.when(step == 0)
+        def _():
+            n_scr[...] = na_ref[...]
+            aux_scr[...] = xa_ref[...].astype(f32)
+
+        @pl.when(step == 1)
+        def _():
+            n_scr[...] = nb_ref[...]
+            aux_scr[...] = xb_ref[...].astype(f32)
+
+        a_scr[...] = nn(n_scr[...], w_ref[...])
+        age_scr[...] = jnp.broadcast_to(aux_scr[:, 0:1], (tokens, LANES))
+
+        def smooth(i, carry):
+            at = pl.ds(pl.multiple_of(i * STRIP, STRIP), STRIP)
+            v = a_scr[at, :] + b_ref[...]
+            cdf = 0.5 + 0.5 * lax.erf(v * 0.7071067811865476)
+            slope = cdf + v * (0.3989422804014327 * jnp.exp(-0.5 * v * v))
+            act = v * cdf
+            value_ref[at, :] = act[:, :units].astype(bf16)
+            gp_ref[at, :] = slope[:, :units].astype(bf16)
+            mask = jnp.broadcast_to(aux_scr[at, 2:3], (STRIP, LANES))
+            z_ref[at, :] = act[:, units:] * mask
+            g2_ref[at, :] = slope[:, units:] * mask
+            return carry
+
+        lax.fori_loop(0, strips, smooth, 0)
+        z = z_ref[...]
+        for b in range(8):
+            shifted[b, :PAD, :] = jnp.zeros((PAD, LANES), f32)
+            shifted[b, PAD:, :] = z if b == 0 else pltpu.roll(z, b, 0)
+        for s in range(strips):
+            age = age_scr[s * STRIP : (s + 1) * STRIP, :]
+
+            def lags(a, acc, s=s, age=age):
+                base = pl.multiple_of(a * 8, 8)
+                left = age - (a * 8).astype(f32)
+                for b in range(8):
+                    row = k_ref[pl.ds(base + b, 1), :]
+                    past = shifted[b, pl.ds(pl.multiple_of(PAD + s * STRIP - base, 8), STRIP), :]
+                    acc = acc + jnp.where(left >= b, past, 0.0) * row
+                return acc
+
+            y_scr[s * STRIP : (s + 1) * STRIP, :] = lax.fori_loop(
+                0, (s + 1) * (STRIP // 8), lags, jnp.zeros((STRIP, LANES), f32)
+            )
+        y_ref[...] = (y_scr[...] + s_ref[...] * z).astype(bf16)
+
+    half = lambda cols: pl.BlockSpec((tokens, cols), lambda i: (i, 0))
+    return pl.pallas_call(
+        kernel,
+        grid=(2,),
+        out_shape=(
+            jax.ShapeDtypeStruct((2 * tokens, units), bf16),
+            jax.ShapeDtypeStruct((2 * tokens, units), bf16),
+            jax.ShapeDtypeStruct((2 * tokens, LANES), f32),
+            jax.ShapeDtypeStruct((2 * tokens, LANES), f32),
+            jax.ShapeDtypeStruct((2 * tokens, LANES), bf16),
+        ),
+        in_specs=[
+            whole((tokens, depth)), whole((tokens, depth)), whole((depth, width)),
+            whole((1, width)), whole(filt.shape), whole((1, LANES)),
+            whole((tokens, LANES)), whole((tokens, LANES)),
+        ],
+        out_specs=(half(units), half(units), half(LANES), half(LANES), half(LANES)),
+        scratch_shapes=[
+            VMEM((tokens, depth), bf16),
+            VMEM((tokens, width), f32),
+            VMEM((tokens, LANES), f32),
+            VMEM((tokens, LANES), f32),
+            VMEM((8, PAD + tokens, LANES), f32),
+            VMEM((tokens, LANES), f32),
+        ],
+        compiler_params=params(),
+        cost_estimate=cost(9.0),
+        name="forward_in",
+    )(na, nb, weight, bias, filt, skip, auxa, auxb)
+
+
+def forward_out(me, ys, expand, bias, value, outw):
+    tokens = ys[0].shape[0] // 2
+    feats, units = expand.shape
+    depth = outw.shape[1]
+
+    def kernel(
+        me_ref, y0, y1, y2, y3, e_ref, b_ref, value_ref, o_ref,
+        c_ref, gated_ref, full_ref, first_ref, second_ref,
+    ):
+        dp = me_ref[0]
+        for k, part in enumerate((y0, y1, y2, y3)):
+            full_ref[:, pl.ds(pl.multiple_of((dp ^ k) * LANES, LANES), LANES)] = part[...]
+        c = nn(full_ref[...], e_ref[...]) + b_ref[...]
+        gated = (c * value_ref[...].astype(f32)).astype(bf16)
+        c_ref[...] = c.astype(bf16)
+        gated_ref[...] = gated
+        out = nn(gated, o_ref[...]).astype(bf16)
+
+        @pl.when(pl.program_id(0) == 0)
+        def _():
+            first_ref[...] = out
+
+        @pl.when(pl.program_id(0) == 1)
+        def _():
+            second_ref[...] = out
+
+    same = lambda cols: pl.BlockSpec((tokens, cols), lambda i: (i, 0))
+    other = lambda cols: pl.BlockSpec((tokens, cols), lambda i: (1 - i, 0))
+    return pl.pallas_call(
+        kernel,
+        grid=(2,),
+        out_shape=(
+            jax.ShapeDtypeStruct((2 * tokens, units), bf16),
+            jax.ShapeDtypeStruct((2 * tokens, units), bf16),
+            jax.ShapeDtypeStruct((2 * tokens, feats), bf16),
+            jax.ShapeDtypeStruct((tokens, depth), bf16),
+            jax.ShapeDtypeStruct((tokens, depth), bf16),
+        ),
+        in_specs=[
+            scalars(), same(LANES), other(LANES), same(LANES), other(LANES),
+            whole((feats, units)), whole((1, units)), same(units), whole((units, depth)),
+        ],
+        out_specs=(same(units), same(units), same(feats), whole((tokens, depth)), whole((tokens, depth))),
+        compiler_params=params(),
+        cost_estimate=cost(3.5),
+        name="forward_out",
+    )(me, *ys, expand, bias, value, outw)
+
+
+def backward_out(me, da, db, outw, expand, value, slope, gate):
+    tokens, depth = da.shape
+    feats, units = expand.shape
+
+    def kernel(
+        me_ref, da_ref, db_ref, o_ref, e_ref, value_ref, gp_ref, c_ref,
+        dc_ref, da1_ref, even_ref, odd_ref, sum_ref, d_scr, y_scr,
+    ):
+        dp = me_ref[0]
+        step = pl.program_id(0)
+
+        @pl.when(step == 0)
+        def _():
+            d_scr[...] = da_ref[...]
+            sum_ref[...] = jnp.zeros_like(sum_ref)
+
+        @pl.when(step == 1)
+        def _():
+            d_scr[...] = db_ref[...]
+
+        dgated = nt(d_scr[...], o_ref[...])
+        dc = (dgated * value_ref[...].astype(f32)).astype(bf16)
+        dc_ref[...] = dc
+        da1_ref[...] = (dgated * c_ref[...].astype(f32) * gp_ref[...].astype(f32)).astype(bf16)
+        sum_ref[...] += jnp.sum(dc.astype(f32), axis=0, keepdims=True)
+        y_scr[...] = nt(dc, e_ref[...])
+        for k, (ref, slot) in enumerate(((even_ref, 0), (odd_ref, 0), (even_ref, 1), (odd_ref, 1))):
+            ref[slot] = y_scr[:, pl.ds(pl.multiple_of((dp ^ k) * LANES, LANES), LANES)].astype(bf16)
+
+    same = lambda cols: pl.BlockSpec((tokens, cols), lambda i: (i, 0))
+    return pl.pallas_call(
+        kernel,
+        grid=(2,),
+        out_shape=(
+            jax.ShapeDtypeStruct((2 * tokens, units), bf16),
+            jax.ShapeDtypeStruct((2 * tokens, units), bf16),
+            jax.ShapeDtypeStruct((2, 2 * tokens, LANES), bf16),
+            jax.ShapeDtypeStruct((2, 2 * tokens, LANES), bf16),
+            jax.ShapeDtypeStruct((1, units), f32),
+        ),
+        in_specs=[
+            scalars(), whole((tokens, depth)), whole((tokens, depth)), whole((units, depth)),
+            whole((feats, units)), same(units), same(units), same(units),
+        ],
+        out_specs=(
+            same(units), same(units),
+            pl.BlockSpec((2, tokens, LANES), lambda i: (0, i, 0)),
+            pl.BlockSpec((2, tokens, LANES), lambda i: (0, 1 - i, 0)),
+            whole((1, units)),
+        ),
+        scratch_shapes=[VMEM((tokens, depth), bf16), VMEM((tokens, feats), f32)],
+        compiler_params=params(),
+        cost_estimate=cost(3.5),
+        name="backward_out",
+    )(me, da, db, outw, expand, value, slope, gate)
+
+
+def backward_in(own, near, far, z, slope2, da1, filt, skip, auxa, auxb, weight):
+    tokens = auxa.shape[0]
+    depth, width = weight.shape
+    units = width - LANES
+    strips = tokens // STRIP
+
+    def kernel(
+        own_ref, near_ref, far_ref, z_ref, g2_ref, da1_ref, k_ref, s_ref, xa_ref, xb_ref, w_ref,
+        da_ref, first_ref, second_ref, corr_ref, sum_ref, skip_ref,
+        aux_scr, rem_scr, shifted, dz_scr,
+    ):
+        step = pl.program_id(0)
+
+        @pl.when(step == 0)
+        def _():
+            aux_scr[...] = xa_ref[...].astype(f32)
+            corr_ref[...] = jnp.zeros_like(corr_ref)
+            sum_ref[...] = jnp.zeros_like(sum_ref)
+            skip_ref[...] = jnp.zeros_like(skip_ref)
+
+        @pl.when(step == 1)
+        def _():
+            aux_scr[...] = xb_ref[...].astype(f32)
+
+        rem_scr[...] = jnp.broadcast_to(aux_scr[:, 1:2], (tokens, LANES))
+        dy = own_ref[0].astype(f32) + near_ref[0].astype(f32) + far_ref[...].astype(f32)
+        for b in range(8):
+            shifted[b, tokens:, :] = jnp.zeros((PAD, LANES), f32)
+            shifted[b, :tokens, :] = dy if b == 0 else pltpu.roll(dy, tokens - b, 0)
+        for s in range(strips):
+            rem = rem_scr[s * STRIP : (s + 1) * STRIP, :]
+            z = z_ref[s * STRIP : (s + 1) * STRIP, :]
+
+            def lags(a, acc, s=s, rem=rem, z=z):
+                base = pl.multiple_of(a * 8, 8)
+                left = rem - (a * 8).astype(f32)
+                for b in range(8):
+                    row = k_ref[pl.ds(base + b, 1), :]
+                    later = shifted[b, pl.ds(pl.multiple_of(s * STRIP + base, 8), STRIP), :]
+                    later = jnp.where(left >= b, later, 0.0)
+                    acc = acc + later * row
+                    pair = later * z
+                    corr_ref[base + b] += (pair[0:8] + pair[8:16]) + (pair[16:24] + pair[24:32])
+                return acc
+
+            dz_scr[s * STRIP : (s + 1) * STRIP, :] = lax.fori_loop(
+                0, (strips - s) * (STRIP // 8), lags, jnp.zeros((STRIP, LANES), f32)
+            )
+        z = z_ref[...]
+        da2 = ((dz_scr[...] + s_ref[...] * dy) * g2_ref[...]).astype(bf16)
+        da_ref[:, :units] = da1_ref[...]
+        da_ref[:, units:] = da2
+        skip_ref[...] += jnp.sum(z * dy, axis=0, keepdims=True)
+        sum_ref[...] += jnp.sum(da_ref[...].astype(f32), axis=0, keepdims=True)
+        out = nt(da_ref[...], w_ref[...]).astype(bf16)
+
+        @pl.when(step == 0)
+        def _():
+            first_ref[...] = out
+
+        @pl.when(step == 1)
+        def _():
+            second_ref[...] = out
+
+    same = lambda cols: pl.BlockSpec((tokens, cols), lambda i: (i, 0))
+    return pl.pallas_call(
+        kernel,
+        grid=(2,),
+        out_shape=(
+            jax.ShapeDtypeStruct((2 * tokens, width), bf16),
+            jax.ShapeDtypeStruct((tokens, depth), bf16),
+            jax.ShapeDtypeStruct((tokens, depth), bf16),
+            jax.ShapeDtypeStruct((tokens, 8, LANES), f32),
+            jax.ShapeDtypeStruct((1, width), f32),
+            jax.ShapeDtypeStruct((1, LANES), f32),
+        ),
+        in_specs=[
+            pl.BlockSpec((1, tokens, LANES), lambda i: (0, i, 0)),
+            pl.BlockSpec((1, tokens, LANES), lambda i: (0, i, 0)),
+            same(LANES), same(LANES), same(LANES), same(units),
+            whole(filt.shape), whole((1, LANES)), whole((tokens, LANES)), whole((tokens, LANES)),
+            whole((depth, width)),
+        ],
+        out_specs=(
+            same(width), whole((tokens, depth)), whole((tokens, depth)),
+            whole((tokens, 8, LANES)), whole((1, width)), whole((1, LANES)),
+        ),
+        scratch_shapes=[
+            VMEM((tokens, LANES), f32),
+            VMEM((tokens, LANES), f32),
+            VMEM((8, PAD + tokens, LANES), f32),
+            VMEM((tokens, LANES), f32),
+        ],
+        compiler_params=params(),
+        cost_estimate=cost(11.0),
+        name="backward_in",
+    )(own, near, far, z, slope2, da1, filt, skip, auxa, auxb, weight)
+
+
+def grads_out(me, gated, douts, full, dc, tall, small):
+    tokens, depth = douts[0].shape
+    units = dc[0].shape[1]
+    feats = full[0].shape[1]
+    thirds = units // 256
+    across = depth // 256
+    rows = tall + small * GROUP * thirds // across
+
+    def kernel(me_ref, g_lo, g_hi, d0, d1, d2, d3, y_lo, y_hi, c_lo, c_hi, *refs):
+        outs, (o_scr, e_scr) = refs[:RINGS], refs[RINGS:]
+        dp, fs = me_ref[0], me_ref[1]
+        step = pl.program_id(0)
+        o_scr[pl.ds(pl.multiple_of(step * 256, 256), 256), :] = (
+            tn(g_lo[:tokens], d0[...])
+            + tn(g_lo[tokens:], d1[...])
+            + tn(g_hi[:tokens], d2[...])
+            + tn(g_hi[tokens:], d3[...])
+        ).astype(bf16)
+        e_scr[step] = (tn(y_lo[...], c_lo[...]) + tn(y_hi[...], c_hi[...])).astype(bf16)
+
+        @pl.when(step == thirds - 1)
+        def _():
+            for j in range(RINGS):
+                outs[j][:tall, :] = o_scr[pl.ds(pl.multiple_of((fs ^ j) * tall, tall), tall), :]
+                for k in range(GROUP):
+                    index = (dp ^ k) * RINGS + (fs ^ j)
+                    at = pl.ds(pl.multiple_of(index * small, small), small)
+                    for t in range(thirds):
+                        r, c = divmod(k * thirds + t, across)
+                        outs[j][
+                            tall + small * r : tall + small * (r + 1), c * 256 : (c + 1) * 256
+                        ] = e_scr[t, at, :]
+
+    column = lambda n: pl.BlockSpec((n, 256), lambda i: (0, i))
+    return pl.pallas_call(
+        kernel,
+        grid=(thirds,),
+        out_shape=(jax.ShapeDtypeStruct((rows, depth), bf16),) * RINGS,
+        in_specs=[scalars()]
+        + [column(2 * tokens)] * 2
+        + [whole((tokens, depth))] * 4
+        + [whole((2 * tokens, feats))] * 2
+        + [column(2 * tokens)] * 2,
+        out_specs=(whole((rows, depth)),) * RINGS,
+        scratch_shapes=[VMEM((units, depth), bf16), VMEM((thirds, feats, 256), bf16)],
+        compiler_params=params(),
+        cost_estimate=cost(5.0),
+        name="grads_out",
+    )(me, *gated, *douts, *full, *dc)
+
+
+def grads_in(me, norms, das, powers, corr, mixing, tall, small):
+    tokens, depth = norms[0].shape
+    width = das[0].shape[1]
+    states = powers.shape[1]
+    rows = tall * GROUP + small
+    wide = depth // GROUP
+
+    def kernel(me_ref, n0, n1, n2, n3, a_lo, a_hi, e_ref, corr_ref, mix_ref, *refs):
+        outs, (dec_ref, w_scr, m_scr) = refs[:RINGS], refs[RINGS:]
+        dp, fs = me_ref[0], me_ref[1]
+        step = pl.program_id(0)
+        w_scr[...] = (
+            tn(n0[...], a_lo[:tokens])
+            + tn(n1[...], a_lo[tokens:])
+            + tn(n2[...], a_hi[:tokens])
+            + tn(n3[...], a_hi[tokens:])
+        ).astype(bf16)
+        spot = pl.ds(pl.multiple_of((step ^ dp) * tall, tall), tall)
+        for j in range(RINGS):
+            outs[j][spot, :] = w_scr[pl.ds(pl.multiple_of((fs ^ j) * tall, tall), tall), :]
+
+        @pl.when(step == 0)
+        def _():
+            corr_f = corr_ref[...]
+            m_scr[...] = tn(e_ref[...], corr_f.astype(bf16)).astype(bf16)
+            lag = lax.broadcasted_iota(jnp.int32, corr_f.shape, 0).astype(f32)
+            dec_ref[...] = -tn(e_ref[...], (corr_f * lag).astype(bf16)) * mix_ref[...].astype(f32)
+            for j in range(RINGS):
+                outs[j][GROUP * tall :, :] = jnp.zeros((small, width), bf16)
+                for k in range(GROUP):
+                    index = (dp ^ k) * RINGS + (fs ^ j)
+                    outs[j][GROUP * tall :, k * LANES : (k + 1) * LANES] = m_scr[
+                        pl.ds(pl.multiple_of(index * small, small), small), :
+                    ]
+
+    return pl.pallas_call(
+        kernel,
+        grid=(GROUP,),
+        out_shape=(jax.ShapeDtypeStruct((rows, width), bf16),) * RINGS
+        + (jax.ShapeDtypeStruct((states, LANES), f32),),
+        in_specs=[scalars()]
+        + [pl.BlockSpec((tokens, wide), lambda i: (0, i))] * 4
+        + [whole((2 * tokens, width))] * 2
+        + [whole(powers.shape), whole(corr.shape), whole(mixing.shape)],
+        out_specs=(whole((rows, width)),) * RINGS + (whole((states, LANES)),),
+        scratch_shapes=[VMEM((wide, width), bf16), VMEM((states, LANES), bf16)],
+        compiler_params=params(),
+        cost_estimate=cost(5.0),
+        name="grads_in",
+    )(me, *norms, *das, powers, corr, mixing)
+
+
+def finish(me, value_parts, expand_parts, out_parts, stateinput, stateoutput):
+    layers, small, states = stateinput.shape
+    rows, width = value_parts[0][0].shape
+    tall = rows - small
+    units = width - LANES
+    high, depth = out_parts[0].shape
+    feats = LANES * GROUP
+
+    def kernel(me_ref, *refs):
+        dp = me_ref[0]
+        count = layers * GROUP
+        values, expands, outs = refs[:count], refs[count : 2 * count], refs[2 * count : 2 * count + layers]
+        si_ref, so_ref, v_ref, r_ref, si_out, so_out, e_ref, o_ref, m_scr = refs[2 * count + layers :]
+        for l in range(layers):
+            for k in range(GROUP):
+                part = values[l * GROUP + k]
+                q = dp ^ k
+                v_ref[l, :, pl.ds(pl.multiple_of(q * units, LANES), units)] = part[:tall, :units].astype(f32)
+                thin = pl.ds(pl.multiple_of(q * LANES, LANES), LANES)
+                r_ref[l, :, thin] = part[:tall, units:].astype(f32)
+                m_scr[:, thin] = part[tall:, k * LANES : (k + 1) * LANES].astype(f32)
+                e_ref[l, :, pl.ds(pl.multiple_of(q * units, LANES), units)] = expands[l * GROUP + k][...].astype(f32)
+            si_out[l] = m_scr[...] * so_ref[l].astype(f32)
+            so_out[l] = m_scr[...] * si_ref[l].astype(f32)
+            o_ref[l] = outs[l][...]
+
+    flat = [p for parts in value_parts for p in parts] + [p for parts in expand_parts for p in parts]
+    arrays = flat + list(out_parts) + [stateinput, stateoutput]
+    return pl.pallas_call(
+        kernel,
+        out_shape=(
+            jax.ShapeDtypeStruct((layers, tall, units * GROUP), f32),
+            jax.ShapeDtypeStruct((layers, tall, feats), f32),
+            jax.ShapeDtypeStruct((layers, small, feats), f32),
+            jax.ShapeDtypeStruct((layers, small, feats), f32),
+            jax.ShapeDtypeStruct((layers, small, units * GROUP), f32),
+            jax.ShapeDtypeStruct((layers, high, depth), f32),
+        ),
+        in_specs=[scalars()] + [pl.BlockSpec(memory_space=VMEM)] * len(arrays),
+        out_specs=(pl.BlockSpec(memory_space=VMEM),) * 6,
+        scratch_shapes=[VMEM((small, feats), f32)],
+        compiler_params=params(),
+        cost_estimate=cost(3.0),
+        name="finish",
+    )(me, *arrays)
+
+
+def after(block, *others):
+    tie = sum(o[(slice(0, 1),) * o.ndim].reshape(1, 1) for o in others)
+    return lax.optimization_barrier((block, tie))[0]
+
+
+def gather_rest(pack):
+    along = [pack] + [swap(pack, 2 * k) for k in range(1, RINGS // 2)]
+    both = []
+    for piece in along:
+        both += [piece, swap(piece, 1)]
+    return both, along[1:]
+
+
+def reduce_rest(packs):
+    summed = [None] * (RINGS // 2)
+    for k in (1, 2, 3, 0):
+        summed[k] = packs[2 * k].astype(f32) + swap(packs[2 * k + 1], 1).astype(f32)
+    total = summed[0]
+    for k in (1, 2, 3):
+        total = total + swap(summed[k].astype(bf16), 2 * k).astype(f32)
+    return total
+
+
+def gather_group(block):
+    near = swap(block, RINGS)
+    far = swap(block, 2 * RINGS)
+    return [block, near, far, swap(far, RINGS)]
+
+
+def return_group(lo, hi):
+    ahead = hi[0].astype(f32) + swap(hi[1], RINGS).astype(f32)
+    there = swap(ahead.astype(bf16), 2 * RINGS)
+    here = lo[0].astype(f32) + swap(lo[1], RINGS).astype(f32)
+    return here + there.astype(f32)
+
+
+def all_rest(block):
+    total = block + sum(swap(block, 2 * k) for k in range(1, RINGS // 2))
+    return total + swap(total, 1)
+
+
+def all_group(block):
+    return block + sum(swap(block, k * RINGS) for k in range(1, GROUP))
 
 
 def mixer(labels, signal, decays, stateinput, stateoutput, skipgain):
@@ -248,7 +857,7 @@
     return (upstream + dcurrent, terms)
 
 
-def local(
+def plain(
     inputs,
     segment_ids,
     token_mask,
@@ -306,6 +915,234 @@
     return (outputs, upstream) + tuple(results)
 
 
+def fast(
+    inputs, segment_ids, token_mask, cotangent, normgain, normbias, valueproj, valuebias,
+    reduceproj, reducebias, decays, stateinput, stateoutput, skipgain, expandproj, expandbias,
+    outproj, outbias,
+):
+    dp, fs = lax.axis_index("dp"), lax.axis_index("fsdp")
+    me = jnp.stack([dp, fs]).astype(jnp.int32)
+    tokens, depth = inputs.shape
+    tall = valueproj.shape[1]
+    small = stateinput.shape[1]
+    high = outproj.shape[1]
+    hidden = valueproj.shape[2]
+    units = hidden // GROUP
+    feats = reduceproj.shape[2]
+    states = feats
+    assert feats == GROUP * LANES
+    devices = GROUP * RINGS
+    flags = token_mask.astype(f32)[:, None]
+
+    zeros = lambda n: jnp.zeros((n,), bf16)
+    rows = []
+    for l in range(LAYERS):
+        rows.append(jnp.concatenate([normgain[l], normbias[l], outbias[l], decays[l], zeros(16)]))
+        rows.append(jnp.concatenate([valuebias[l], reducebias[l], skipgain[l]]))
+        rows.append(jnp.concatenate([expandbias[l], zeros(32)]))
+    rows += [zeros(LANES)] * 2
+    small_pack = jnp.stack(rows)
+    stacked = jnp.stack([small_pack] + [swap(small_pack, k * RINGS) for k in range(1, GROUP)])
+    stacked = jnp.stack([stacked] + [swap(stacked, 2 * k) for k in range(1, RINGS // 2)])
+    stacked = jnp.stack([stacked, swap(stacked, 1)], axis=1)
+    number = jnp.arange(devices)
+    place = (fs ^ (number % RINGS)) * GROUP + (dp ^ (number // RINGS))
+    pick = (place[:, None] == number[None, :]).astype(bf16)
+    table = nn(pick, stacked.reshape(devices, -1)).reshape(devices, 8, LANES)
+
+    def vector(row, start, stop):
+        return table[:, row, start:stop].reshape(1, -1)
+
+    def quarter(row, start, stop):
+        mine = lax.dynamic_slice_in_dim(table, dp * RINGS, RINGS, 0)
+        return mine[:, row, start:stop].reshape(1, -1)
+
+    gains = [vector(3 * l, 0, 32) for l in range(LAYERS)]
+    shifts = [vector(3 * l, 32, 64) for l in range(LAYERS)]
+    outbiases = [vector(3 * l, 64, 96) for l in range(LAYERS)]
+    rates = [vector(3 * l, 96, 112) for l in range(LAYERS)]
+    inbiases = [
+        jnp.concatenate([quarter(3 * l + 1, 0, 96), quarter(3 * l + 1, 96, 112)], axis=1)
+        for l in range(LAYERS)
+    ]
+    skips = [quarter(3 * l + 1, 112, 128) for l in range(LAYERS)]
+    gatebiases = [quarter(3 * l + 2, 0, 96) for l in range(LAYERS)]
+
+    value_packs, out_packs = [], []
+    for l in range(LAYERS):
+        mixing = (stateinput[l].astype(f32) * stateoutput[l].astype(f32)).astype(bf16)
+        pieces, expands = [], []
+        for k in range(GROUP):
+            q = dp ^ k
+            top = jnp.concatenate(
+                [
+                    lax.dynamic_slice_in_dim(valueproj[l], q * units, units, 1),
+                    lax.dynamic_slice_in_dim(reduceproj[l], q * LANES, LANES, 1),
+                ],
+                axis=1,
+            )
+            thin = lax.dynamic_slice_in_dim(mixing, q * LANES, LANES, 1)
+            piece = jnp.concatenate([top, jnp.pad(thin, ((0, 0), (0, units)))], axis=0)
+            expand = lax.dynamic_slice_in_dim(expandproj[l], q * units, units, 1)
+            pieces.append(swap(piece, k * RINGS) if k else piece)
+            expands.append(swap(expand, k * RINGS) if k else expand)
+        last = jnp.concatenate(
+            [p[tall:, :LANES] for p in pieces] + [jnp.zeros((small, units - 3 * LANES), bf16)], axis=1
+        )
+        value_packs.append(jnp.concatenate([p[:tall] for p in pieces] + [last], axis=0))
+        blocks = [e[:, t * 256 : (t + 1) * 256] for e in expands for t in range(units // 256)]
+        across = depth // 256
+        strips = [
+            jnp.concatenate(blocks[r : r + across], axis=1) for r in range(0, len(blocks), across)
+        ]
+        out_packs.append(jnp.concatenate([outproj[l]] + strips, axis=0))
+
+    lagged = jnp.arange(tokens, dtype=f32)
+    powers = [jnp.exp(-lagged[:, None] * rates[l]).astype(bf16) for l in range(LAYERS)]
+
+    value_w, mixes, filters, out_w, expand_w = [], [], [], [], []
+    behind = ()
+    for l in range(LAYERS):
+        parts, marks = gather_rest(after(value_packs[l], *behind) if behind else value_packs[l])
+        w, mix, filt = open_value(me, powers[l], parts)
+        value_w.append(w)
+        mixes.append(mix)
+        filters.append(filt)
+        parts, behind = gather_rest(after(out_packs[l], *marks))
+        o, e = open_out(me, parts, high, small, units)
+        out_w.append(o)
+        expand_w.append(e)
+
+    same = (segment_ids[:, None] == segment_ids[None, :]).astype(f32)
+    spot = jnp.arange(tokens)
+    before = (spot[None, :] < spot[:, None]).astype(f32)
+    age = jnp.sum(same * before, axis=1)
+    rest = jnp.sum(same * (1.0 - before), axis=1) - 1.0
+    aux = jnp.pad(jnp.stack([age, rest, token_mask.astype(f32)], axis=1), ((0, 0), (0, LANES - 3)))
+    auxes = gather_group(aux.astype(bf16))
+
+    upstream = cotangent.astype(f32)
+    dout = (flags * upstream).astype(bf16)
+    douts = gather_group(dout)
+
+    current = inputs.astype(f32)
+    saved = []
+    for l in range(LAYERS):
+        center = current - jnp.mean(current, axis=1, keepdims=True)
+        rstd = lax.rsqrt(jnp.mean(center * center, axis=1, keepdims=True) + 1e-05)
+        normed = center * rstd
+        norms = gather_group((normed * gains[l] + shifts[l]).astype(bf16))
+        lo = forward_in(*norms[:2], value_w[l], inbiases[l], filters[l], skips[l], *auxes[:2])
+        hi = forward_in(*norms[2:], value_w[l], inbiases[l], filters[l], skips[l], *auxes[2:])
+        y_lo, y_hi = lo[4], hi[4]
+        far_lo, far_hi = swap(y_lo, 2 * RINGS), swap(y_hi, 2 * RINGS)
+        out_hi = forward_out(
+            me, (y_hi, swap(y_hi, RINGS), far_lo, swap(far_lo, RINGS)),
+            expand_w[l], gatebiases[l], hi[0], out_w[l],
+        )
+        out_lo = forward_out(
+            me, (y_lo, swap(y_lo, RINGS), far_hi, swap(far_hi, RINGS)),
+            expand_w[l], gatebiases[l], lo[0], out_w[l],
+        )
+        branch = return_group(out_lo[3:], out_hi[3:]) + outbiases[l]
+        current = current + flags * branch
+        saved.append((normed, rstd, norms, lo, hi, out_lo, out_hi))
+    outputs = current.astype(bf16)
+
+    value_grads, out_grads, sums_all, sums_rest = [None] * 2, [None] * 2, [None] * 2, [None] * 2
+    for l in reversed(range(LAYERS)):
+        normed, rstd, norms, lo, hi, out_lo, out_hi = saved[l]
+        if l < LAYERS - 1:
+            dout = (flags * upstream).astype(bf16)
+            douts = gather_group(dout)
+        back_lo = backward_out(me, *douts[:2], out_w[l], expand_w[l], lo[0], lo[1], out_lo[0])
+        near_lo = swap(back_lo[3], RINGS)
+        far_lo = swap((back_lo[2][1].astype(f32) + near_lo[1].astype(f32)).astype(bf16), 2 * RINGS)
+        back_hi = backward_out(me, *douts[2:], out_w[l], expand_w[l], hi[0], hi[1], out_hi[0])
+        near_hi = swap(back_hi[3], RINGS)
+        far_hi = swap((back_hi[2][1].astype(f32) + near_hi[1].astype(f32)).astype(bf16), 2 * RINGS)
+        in_hi = backward_in(
+            back_hi[2], near_hi, far_lo, hi[2], hi[3], back_hi[1], filters[l], skips[l], *auxes[2:], value_w[l]
+        )
+        in_lo = backward_in(
+            back_lo[2], near_lo, far_hi, lo[2], lo[3], back_lo[1], filters[l], skips[l], *auxes[:2], value_w[l]
+        )
+        dnrm = return_group(in_lo[1:3], in_hi[1:3])
+        out_grads[l] = reduce_rest(
+            grads_out(
+                me, (out_lo[1], out_hi[1]), douts, (out_lo[2], out_hi[2]), (back_lo[0], back_hi[0]), high, small
+            )
+        )
+        corr = jnp.sum(in_lo[3] + in_hi[3], axis=1)
+        *packs, terms = grads_in(me, norms, (in_lo[0], in_hi[0]), powers[l], corr, mixes[l], tall, small)
+        value_grads[l] = reduce_rest(packs)
+        gain_term = jnp.sum(dnrm * normed, axis=0)
+        shift_term = jnp.sum(dnrm, axis=0)
+        out_term = jnp.sum(dout.astype(f32), axis=0)
+        q = dnrm * gains[l]
+        slope = q - jnp.mean(q, axis=1, keepdims=True) - normed * jnp.mean(q * normed, axis=1, keepdims=True)
+        upstream = upstream + slope * rstd
+        sums_all[l] = jnp.concatenate([gain_term, shift_term, out_term, jnp.sum(terms, axis=1)]).reshape(-1, LANES)
+        sums_rest[l] = jnp.concatenate(
+            [
+                (in_lo[4] + in_hi[4]).reshape(-1, LANES),
+                (back_lo[4] + back_hi[4]).reshape(-1, LANES),
+                in_lo[5] + in_hi[5],
+            ]
+        )
+
+    pieces, expands, outs = [], [], []
+    for l in range(LAYERS):
+        g = value_grads[l]
+        parts = []
+        for k in range(GROUP):
+            part = jnp.concatenate([g[k * tall : (k + 1) * tall], g[GROUP * tall :]], axis=0).astype(bf16)
+            parts.append(swap(part, k * RINGS) if k else part)
+        pieces.append(parts)
+        g = out_grads[l]
+        parts = []
+        for k in range(GROUP):
+            blocks = []
+            for t in range(units // 256):
+                r, c = divmod(k * (units // 256) + t, depth // 256)
+                blocks.append(g[high + small * r : high + small * (r + 1), c * 256 : (c + 1) * 256])
+            part = jnp.concatenate(blocks, axis=1).astype(bf16)
+            parts.append(swap(part, k * RINGS) if k else part)
+        expands.append(parts)
+        outs.append(g[:high])
+    valueproj_grad, reduceproj_grad, stateinput_grad, stateoutput_grad, expandproj_grad, outproj_grad = finish(
+        me, pieces, expands, outs, stateinput, stateoutput
+    )
+
+    vectors = []
+    for l in range(LAYERS):
+        head = sums_all[l].shape[0]
+        packed = all_rest(jnp.pad(jnp.concatenate([sums_all[l], sums_rest[l]]), ((0, 6), (0, 0))))
+        shared = all_group(packed[:head]).reshape(-1)
+        mine = packed[head:].reshape(-1)
+        index = dp * RINGS + fs
+        take = lambda array, start, n, at: lax.dynamic_slice_in_dim(array, start + at * n, n, 0)
+        vectors.append(
+            (
+                take(shared, 0, depth // devices, index),
+                take(shared, depth, depth // devices, index),
+                take(mine, 0, units // RINGS, fs),
+                take(mine, units, LANES // RINGS, fs),
+                take(shared, 3 * depth, states // devices, index),
+                take(mine, 2 * units + LANES, LANES // RINGS, fs),
+                take(mine, units + LANES, units // RINGS, fs),
+                take(shared, 2 * depth, depth // devices, index),
+            )
+        )
+    gain_g, shift_g, vbias_g, rbias_g, decays_g, skip_g, ebias_g, obias_g = (
+        jnp.stack([vectors[l][i] for l in range(LAYERS)]) for i in range(8)
+    )
+    return (
+        outputs, upstream, gain_g, shift_g, valueproj_grad, vbias_g, reduceproj_grad, rbias_g, decays_g,
+        stateinput_grad, stateoutput_grad, skip_g, expandproj_grad, ebias_g, outproj_grad, obias_g,
+    )
+
+
 def solution(mesh):
     placed = (
         P(("dp", "fsdp"), None),
@@ -327,8 +1164,9 @@
         P(None, ("dp", "fsdp"), None),
         P(None, ("dp", "fsdp")),
     )
+    small = mesh.shape["dp"] == GROUP and mesh.shape["fsdp"] == RINGS
     return jax.shard_map(
-        local,
+        fast if small else plain,
         mesh=mesh,
         in_specs=placed,
         out_specs=(

time: 2820 us -> 569 us (0.20)
  waiting for transfers between devices: 1750 us -> 180 us
  blocking collectives: 319 us -> 0 us
  matrix products: 317 us -> 0.21 us
  other arithmetic: 207 us -> 37.3 us
  Pallas kernels: 0 us -> 150 us
  starting transfers between devices: 1.1 us -> 127 us
  local copies, waits for them, and re-layouts: 152 us -> 64.5 us
  loops' own time: 44.8 us -> 0 us
    reduce_scatter x12 -> x0, waiting for transfers between devices: 1670 us -> none  [the longest x2 320 us: scatter_layer(): lax.psum_scatter(terms[12], ('dp', 'fsdp'), scatter_dimension=0, tiled=True)]
    dot_general x126 -> x1, matrix products: 317 us -> 0.21 us  [nn(): return jnp.dot(a, b, preferred_element_type=f32)]
    all_gather x4 -> x0, blocking collectives: 276 us -> none  [the longest x2 141 us: gather_forward(): lax.all_gather(shards[7][depth], ('dp', 'fsdp'), axis=0, tiled=True)]
    ppermute x0 -> x148, waiting for transfers between devices: none -> 180 us  [swap(): return lax.ppermute(block, AXES, [(i, i ^ flip) for i in range(size)])]
    pallas_call x0 -> x25, Pallas kernels: none -> 150 us  [the longest x4 53.2 us: backward_in(): pl.pallas_call(kernel, grid=(2,), out_shape=(jax.ShapeDtypeStruct((2 * to...]
    ppermute x0 -> x148, starting transfers between devices: none -> 127 us  [swap(): return lax.ppermute(block, AXES, [(i, i ^ flip) for i in range(size)])]
    unnamed x22 -> x0, waiting for transfers between devices: 70.4 us -> none
    reduce_sum x41 -> x12, other arithmetic: 81.8 us -> 12.3 us  [the longest x2 6.37 us: fast(): out_term = jnp.sum(dout.astype(f32), axis=0)]
  transfers between devices with their start and end apart: 21 -> 148, of which waited for: 14 -> 49; matrix products, arithmetic and copies ran while one was open for 9% -> 10% of each run, Pallas kernels for 0% -> 27%
where the time goes in v1:
time: 569 us; the launch traced here: 563 us
  waiting for transfers between devices  180 us (32%)
  Pallas kernels  150 us (26%)
  starting transfers between devices  127 us (22%)
  local copies, waits for them, and re-layouts  64.5 us (11%)
  other arithmetic  37.3 us (7%)
    ppermute x148, waiting for transfers between devices, swap(): return lax.ppermute(block, AXES, [(i, i ^ flip) for i in range(size)])  180 us
    ppermute x148, starting transfers between devices, swap(): return lax.ppermute(block, AXES, [(i, i ^ flip) for i in range(size)])  127 us
    pallas_call x4, Pallas kernels, backward_in(): pl.pallas_call(kernel, grid=(2,), out_shape=(jax.ShapeDtypeStruct((2 * to...  53.2 us
    unnamed x368, local copies, waits for them, and re-layouts  43.5 us
    pallas_call x4, Pallas kernels, forward_in(): pl.pallas_call(kernel, grid=(2,), out_shape=(jax.ShapeDtypeStruct((2 * to...  38.4 us
    pallas_call x4, Pallas kernels, backward_out(): pl.pallas_call(kernel, grid=(2,), out_shape=(jax.ShapeDtypeStruct((2 * to...  17.4 us
    pallas_call x4, Pallas kernels, forward_out(): pl.pallas_call(kernel, grid=(2,), out_shape=(jax.ShapeDtypeStruct((2 * to...  13.8 us
  transfers between devices with their start and end apart: 148, of which 49 were waited for; matrix products, arithmetic and copies ran while one was open for 10% of the time, Pallas kernels for 27%

profile of v1, /device:TPU:0, one launch (start us, length us, event | category | flops | bytes accessed | tf_op | source)
XLA Modules:
  0.0 563.1 jit_solution(7711573904731857067)
XLA Ops:
  58.2 8.4 %collective-permute-done.14.refs_4_ = bf16[144,896]{1,0:T(8,128)(2,1)S(1)} collective-permute-done((bf16[144,896]{1,0:T(8,128)(2,1)S(1)}, bf16[144,896]{1,0:T(8,128)(2,1)S(1)}, u32[]{:S(2)}, u32[]{:S(2)}) %collective-permute-start.14) | collective-permute-done | bytes 258080 | tf_op jit(solution)/shard_map/ppermute | solution.py:29
  75.7 5.4 collective-permute-done.15.refs_5_
  89.9 9.5 %forward_in.4 = (bf16[512,768]{1,0:T(8,128)(2,1)S(1)}, bf16[512,768]{1,0:T(8,128)(2,1)S(1)}, f32[512,128]{1,0:T(8,128)S(1)}, f32[512,128]{1,0:T(8,128)S(1)}, bf16[512,128]{1,0:T(8,128)(2,1)S(1)}) custom-call(bf16[256,1024]{1,0:T(8,128)(2,1)S(1)} %fusion.7.na_ref.n0, bf16[256,1024]{1,0:T(8,128)(2,1)S(1)} %collective-permute-done.7.nb_ref.n1, ...), custom_call_target="tpu_custom_call" | custom-call | flops 8999999488 | bytes 1048576 | tf_op jit(solution)/shard_map/forward_in/pallas_call | solution.py:195
  110.1 9.3 %forward_in.5 = (bf16[512,768]{1,0:T(8,128)(2,1)S(1)}, bf16[512,768]{1,0:T(8,128)(2,1)S(1)}, f32[512,128]{1,0:T(8,128)S(1)}, f32[512,128]{1,0:T(8,128)S(1)}, bf16[512,128]{1,0:T(8,128)(2,1)S(1)}) custom-call(bf16[256,1024]{1,0:T(8,128)(2,1)S(1)} %collective-permute-done.20.na_ref.n2, bf16[256,1024]{1,0:T(8,128)(2,1)S(1)} %collective-permute-done.21.nb_ref.n3, ...), custom_call_target="tpu_custom_call" | custom-call | flops 8999999488 | bytes 1048576 | tf_op jit(solution)/shard_map/forward_in/pallas_call | solution.py:195
  124.7 4.9 collective-permute-done.35.refs_7_
  154.1 4.6 collective-permute-done.47.refs_2_
  158.7 9.4 %collective-permute-done.49.refs_4_ = bf16[144,896]{1,0:T(8,128)(2,1)} collective-permute-done((bf16[144,896]{1,0:T(8,128)(2,1)S(1)}, bf16[144,896]{1,0:T(8,128)(2,1)}, u32[]{:S(2)}, u32[]{:S(2)}) %collective-permute-start.49) | collective-permute-done | bytes 258080 | tf_op jit(solution)/shard_map/ppermute | solution.py:29
  195.6 15.4 %collective-permute-done.64.refs_4_ = bf16[144,1024]{1,0:T(8,128)(2,1)S(1)} collective-permute-done((bf16[144,1024]{1,0:T(8,128)(2,1)S(1)}, bf16[144,1024]{1,0:T(8,128)(2,1)S(1)}, u32[]{:S(2)}, u32[]{:S(2)}) %collective-permute-start.64) | collective-permute-done | bytes 294944 | tf_op jit(solution)/shard_map/ppermute | solution.py:29
  214.2 9.3 %forward_in.6 = (bf16[512,768]{1,0:T(8,128)(2,1)S(1)}, bf16[512,768]{1,0:T(8,128)(2,1)S(1)}, f32[512,128]{1,0:T(8,128)S(1)}, f32[512,128]{1,0:T(8,128)S(1)}, bf16[512,128]{1,0:T(8,128)(2,1)S(1)}) custom-call(bf16[256,1024]{1,0:T(8,128)(2,1)S(1)} %add_convert_fusion.4.na_ref.n0, bf16[256,1024]{1,0:T(8,128)(2,1)S(1)} %collective-permute-done.42.nb_ref.n1, ...), custom_call_target="tpu_custom_call" | custom-call | flops 8999999488 | bytes 1048576 | tf_op jit(solution)/shard_map/forward_in/pallas_call | solution.py:195
  225.6 10.3 %forward_in.7 = (bf16[512,768]{1,0:T(8,128)(2,1)S(1)}, bf16[512,768]{1,0:T(8,128)(2,1)S(1)}, f32[512,128]{1,0:T(8,128)S(1)}, f32[512,128]{1,0:T(8,128)S(1)}, bf16[512,128]{1,0:T(8,128)(2,1)S(1)}) custom-call(bf16[256,1024]{1,0:T(8,128)(2,1)} %collective-permute-done.54.na_ref.n2, bf16[256,1024]{1,0:T(8,128)(2,1)S(1)} %collective-permute-done.55.nb_ref.n3, ...), custom_call_target="tpu_custom_call" | custom-call | flops 8999999488 | bytes 1048576 | tf_op jit(solution)/shard_map/forward_in/pallas_call | solution.py:195
  268.8 5.4 grads_out.3
  278.9 13.8 %backward_in.4 = (bf16[512,896]{1,0:T(8,128)(2,1)S(1)}, bf16[256,1024]{1,0:T(8,128)(2,1)S(1)}, bf16[256,1024]{1,0:T(8,128)(2,1)}, f32[256,8,128]{2,1,0:T(8,128)S...) custom-call(bf16[2,512,128]{2,1,0:T(8,128)(2,1)S(1)} %get-tuple-element.176.own_ref, ...), custom_call_target="tpu_custom_call" | custom-call | flops 11000000512 | bytes 1048576 | tf_op jit(solution)/shard_map/backward_in/pallas_call | solution.py:396
  304.6 13.0 %backward_in.5 = (bf16[512,896]{1,0:T(8,128)(2,1)S(1)}, bf16[256,1024]{1,0:T(8,128)(2,1)S(1)}, bf16[256,1024]{1,0:T(8,128)(2,1)S(1)}, f32[256,8,128]{2,1,0:T(8,1...) custom-call(bf16[2,512,128]{2,1,0:T(8,128)(2,1)S(1)} %get-tuple-element.180.own_ref, ...), custom_call_target="tpu_custom_call" | custom-call | flops 11000000512 | bytes 1048576 | tf_op jit(solution)/shard_map/backward_in/pallas_call | solution.py:396
  319.9 5.5 grads_in.3
  359.5 13.8 %collective-permute-done.122 = bf16[144,896]{1,0:T(8,128)(2,1)S(1)} collective-permute-done((bf16[144,896]{1,0:T(8,128)(2,1)S(1)}, bf16[144,896]{1,0:T(8,128)(2,1)S(1)}, u32[]{:S(2)}, u32[]{:S(2)}) %collective-permute-start.122) | collective-permute-done | bytes 258080 | tf_op jit(solution)/shard_map/ppermute | solution.py:29
  414.4 5.4 grads_out.2
  424.5 13.1 %backward_in.7 = (bf16[512,896]{1,0:T(8,128)(2,1)S(1)}, bf16[256,1024]{1,0:T(8,128)(2,1)S(1)}, bf16[256,1024]{1,0:T(8,128)(2,1)S(1)}, f32[256,8,128]{2,1,0:T(8,1...) custom-call(bf16[2,512,128]{2,1,0:T(8,128)(2,1)S(1)} %get-tuple-element.198.own_ref, ...), custom_call_target="tpu_custom_call" | custom-call | flops 11000000512 | bytes 1048576 | tf_op jit(solution)/shard_map/backward_in/pallas_call | solution.py:396
  446.3 13.2 %backward_in.6 = (bf16[512,896]{1,0:T(8,128)(2,1)S(1)}, bf16[256,1024]{1,0:T(8,128)(2,1)S(1)}, bf16[256,1024]{1,0:T(8,128)(2,1)S(1)}, f32[256,8,128]{2,1,0:T(8,1...) custom-call(bf16[2,512,128]{2,1,0:T(8,128)(2,1)S(1)} %get-tuple-element.194.own_ref, ...), custom_call_target="tpu_custom_call" | custom-call | flops 11000000512 | bytes 1048576 | tf_op jit(solution)/shard_map/backward_in/pallas_call | solution.py:396
  461.8 5.0 grads_in.2
  477.1 4.6 collective-permute-done.109
  487.6 5.2 collective-permute-done.113
  498.8 13.1 %collective-permute-done.112 = bf16[144,896]{1,0:T(8,128)(2,1)S(1)} collective-permute-done((bf16[144,896]{1,0:T(8,128)(2,1)S(1)}, bf16[144,896]{1,0:T(8,128)(2,1)S(1)}, u32[]{:S(2)}, u32[]{:S(2)}) %collective-permute-start.112) | collective-permute-done | bytes 258080 | tf_op jit(solution)/shard_map/ppermute | solution.py:29
  519.9 10.8 %collective-permute-done.136.refs_10_ = bf16[16,768]{1,0:T(8,128)(2,1)S(1)} collective-permute-done((bf16[16,768]{1,0:T(8,128)(2,1)S(1)}, bf16[16,768]{1,0:T(8,128)(2,1)S(1)}, u32[]{:S(2)}, u32[]{:S(2)}) %collective-permute-start.136) | collective-permute-done | bytes 24608 | tf_op jit(solution)/shard_map/ppermute | solution.py:29
  540.2 5.5 collective-permute-start.94
  (854 shorter events, 345.7 us)
Async XLA Ops:
  13.3 33.0 %collective-permute-start.43 = (bf16[48,896]{1,0:T(8,128)(2,1)}, bf16[48,896]{1,0:T(8,128)(2,1)}, u32[]{:S(2)}, u32[]{:S(2)}) collective-permute-start(bf16[48,896]{1,0:T(8,128)(2,1)} %fusion.31), channel_id=1, source_target_pairs={{0,8},{1,9},{2,10},{3,11},{4,12},{5,13},{6,14},{7,15},{8,0},{9,1},... | collective-permute-start | bytes 258056 | tf_op jit(solution)/shard_map/ppermute | solution.py:29
  14.1 36.6 %collective-permute-start.44 = (bf16[48,896]{1,0:T(8,128)(2,1)}, bf16[48,896]{1,0:T(8,128)(2,1)}, u32[]{:S(2)}, u32[]{:S(2)}) collective-permute-start(bf16[48,896]{1,0:T(8,128)(2,1)} %fusion.32), channel_id=1, source_target_pairs={{0,16},{1,17},{2,18},{3,19},{4,20},{5,21},{6,22},{7,23},{8,24},{9,... | collective-permute-start | bytes 258056 | tf_op jit(solution)/shard_map/ppermute | solution.py:29
  53.1 36.3 %collective-permute-start.7 = (bf16[256,1024]{1,0:T(8,128)(2,1)S(1)}, bf16[256,1024]{1,0:T(8,128)(2,1)S(1)}, u32[]{:S(2)}, u32[]{:S(2)}) collective-permute-start(bf16[256,1024]{1,0:T(8,128)(2,1)S(1)} %fusion.7.na_ref.n0), channel_id=1, source_target_pairs={{0,8},{1,9},{2,10},{3,11},{4,12},{5,13},{6,14},{7,15},{8,0},{9,1},... | collective-permute-start | bytes 1572872 | tf_op jit(solution)/shard_map/ppermute | solution.py:29
  57.6 31.7 %collective-permute-start.20 = (bf16[256,1024]{1,0:T(8,128)(2,1)S(1)}, bf16[256,1024]{1,0:T(8,128)(2,1)S(1)}, u32[]{:S(2)}, u32[]{:S(2)}) collective-permute-start(bf16[256,1024]{1,0:T(8,128)(2,1)S(1)} %fusion.7.na_ref.n0), channel_id=1, source_target_pairs={{0,16},{1,17},{2,18},{3,19},{4,20},{5,21},{6,22},{7,23},{8,24},{9,... | collective-permute-start | bytes 1572872 | tf_op jit(solution)/shard_map/ppermute | solution.py:29
  121.1 26.4 %collective-permute-start.59 = (bf16[16,768]{1,0:T(8,128)(2,1)}, bf16[16,768]{1,0:T(8,128)(2,1)S(1)}, u32[]{:S(2)}, u32[]{:S(2)}) collective-permute-start(bf16[16,768]{1,0:T(8,128)(2,1)} %get-tuple-element.356), channel_id=1, source_target_pairs={{0,16},{1,17},{2,18},{3,19},{4,20},{5,21},{6,22},{7,23},{8,24},{9,... | collective-permute-start | bytes 73736 | tf_op jit(solution)/shard_map/ppermute | solution.py:29
  144.0 26.2 %collective-permute-start.36 = (bf16[256,1024]{1,0:T(8,128)(2,1)S(1)}, bf16[256,1024]{1,0:T(8,128)(2,1)}, u32[]{:S(2)}, u32[]{:S(2)}) collective-permute-start(bf16[256,1024]{1,0:T(8,128)(2,1)S(1)} %get-tuple-element.158), channel_id=1, source_target_pairs={{0,8},{1,9},{2,10},{3,11},{4,12},{5,13},{6,14},{7,15},{8,0},{9,1},... | collective-permute-start | bytes 1572872 | tf_op jit(solution)/shard_map/ppermute | solution.py:29
  144.6 27.1 %collective-permute-start.41 = (bf16[256,1024]{1,0:T(8,128)(2,1)S(1)}, bf16[256,1024]{1,0:T(8,128)(2,1)}, u32[]{:S(2)}, u32[]{:S(2)}) collective-permute-start(bf16[256,1024]{1,0:T(8,128)(2,1)S(1)} %add_convert_fusion.5), channel_id=1, source_target_pairs={{0,16},{1,17},{2,18},{3,19},{4,20},{5,21},{6,22},{7,23},{8,24},{9,... | collective-permute-start | bytes 1572872 | tf_op jit(solution)/shard_map/ppermute | solution.py:29
  175.4 37.7 %collective-permute-start.42 = (bf16[256,1024]{1,0:T(8,128)(2,1)S(1)}, bf16[256,1024]{1,0:T(8,128)(2,1)S(1)}, u32[]{:S(2)}, u32[]{:S(2)}) collective-permute-start(bf16[256,1024]{1,0:T(8,128)(2,1)S(1)} %add_convert_fusion.4.na_ref.n0), channel_id=1, source_target_pairs={{0,8},{1,9},{2,10},{3,11},{4,12},{5,13},{6,14},{7,15},{8,0},{9,1},... | collective-permute-start | bytes 1572872 | tf_op jit(solution)/shard_map/ppermute | solution.py:29
  178.0 36.1 %collective-permute-start.54 = (bf16[256,1024]{1,0:T(8,128)(2,1)S(1)}, bf16[256,1024]{1,0:T(8,128)(2,1)}, u32[]{:S(2)}, u32[]{:S(2)}) collective-permute-start(bf16[256,1024]{1,0:T(8,128)(2,1)S(1)} %add_convert_fusion.4.na_ref.n0), channel_id=1, source_target_pairs={{0,16},{1,17},{2,18},{3,19},{4,20},{5,21},{6,22},{7,23},{8,24},{9,... | collective-permute-start | bytes 1572872 | tf_op jit(solution)/shard_map/ppermute | solution.py:29
  195.1 28.5 %collective-permute-start.61 = (bf16[144,1024]{1,0:T(8,128)(2,1)S(1)}, bf16[144,1024]{1,0:T(8,128)(2,1)S(1)}, u32[]{:S(2)}, u32[]{:S(2)}) collective-permute-start(bf16[144,1024]{1,0:T(8,128)(2,1)S(1)} %maximum_maximum_fusion.1.refs_0_), channel_id=1, source_target_pairs={{0,1},{1,0},{2,3},{3,2},{4,5},{5,4},{6,7},{7,6},{8,9},{9,8},{10,11... | collective-permute-start | bytes 884744 | tf_op jit(solution)/shard_map/ppermute | solution.py:29
  211.1 29.6 %collective-permute-start.63 = (bf16[144,1024]{1,0:T(8,128)(2,1)S(1)}, bf16[144,1024]{1,0:T(8,128)(2,1)S(1)}, u32[]{:S(2)}, u32[]{:S(2)}) collective-permute-start(bf16[144,1024]{1,0:T(8,128)(2,1)S(1)} %collective-permute-done.62.refs_2_), channel_id=1, source_target_pairs={{0,1},{1,0},{2,3},{3,2},{4,5},{5,4},{6,7},{7,6},{8,9},{9,8},{10,11... | collective-permute-start | bytes 884744 | tf_op jit(solution)/shard_map/ppermute | solution.py:29
  212.1 29.1 %collective-permute-start.65 = (bf16[144,1024]{1,0:T(8,128)(2,1)S(1)}, bf16[144,1024]{1,0:T(8,128)(2,1)S(1)}, u32[]{:S(2)}, u32[]{:S(2)}) collective-permute-start(bf16[144,1024]{1,0:T(8,128)(2,1)S(1)} %collective-permute-done.64.refs_4_), channel_id=1, source_target_pairs={{0,1},{1,0},{2,3},{3,2},{4,5},{5,4},{6,7},{7,6},{8,9},{9,8},{10,11... | collective-permute-start | bytes 884744 | tf_op jit(solution)/shard_map/ppermute | solution.py:29
  213.1 28.1 %collective-permute-start.67 = (bf16[144,1024]{1,0:T(8,128)(2,1)S(1)}, bf16[144,1024]{1,0:T(8,128)(2,1)S(1)}, u32[]{:S(2)}, u32[]{:S(2)}) collective-permute-start(bf16[144,1024]{1,0:T(8,128)(2,1)S(1)} %collective-permute-done.66.refs_6_), channel_id=1, source_target_pairs={{0,1},{1,0},{2,3},{3,2},{4,5},{5,4},{6,7},{7,6},{8,9},{9,8},{10,11... | collective-permute-start | bytes 884744 | tf_op jit(solution)/shard_map/ppermute | solution.py:29
  249.8 50.5 %collective-permute-start.72 = (bf16[256,1024]{1,0:T(8,128)(2,1)S(1)}, bf16[256,1024]{1,0:T(8,128)(2,1)}, u32[]{:S(2)}, u32[]{:S(2)}) collective-permute-start(bf16[256,1024]{1,0:T(8,128)(2,1)S(1)} %get-tuple-element.173), channel_id=1, source_target_pairs={{0,8},{1,9},{2,10},{3,11},{4,12},{5,13},{6,14},{7,15},{8,0},{9,1},... | collective-permute-start | bytes 1572872 | tf_op jit(solution)/shard_map/ppermute | solution.py:29
  277.9 55.0 %collective-permute-start.138 = (bf16[144,1024]{1,0:T(8,128)(2,1)}, bf16[144,1024]{1,0:T(8,128)(2,1)}, u32[]{:S(2)}, u32[]{:S(2)}) collective-permute-start(bf16[144,1024]{1,0:T(8,128)(2,1)} %get-tuple-element.271), channel_id=1, source_target_pairs={{0,1},{1,0},{2,3},{3,2},{4,5},{5,4},{6,7},{7,6},{8,9},{9,8},{10,11... | collective-permute-start | bytes 884744 | tf_op jit(solution)/shard_map/ppermute | solution.py:29
  292.8 82.9 %collective-permute-start.80 = (bf16[256,1024]{1,0:T(8,128)(2,1)}, bf16[256,1024]{1,0:T(8,128)(2,1)}, u32[]{:S(2)}, u32[]{:S(2)}) collective-permute-start(bf16[256,1024]{1,0:T(8,128)(2,1)} %get-tuple-element.186), channel_id=1, source_target_pairs={{0,8},{1,9},{2,10},{3,11},{4,12},{5,13},{6,14},{7,15},{8,0},{9,1},... | collective-permute-start | bytes 1572872 | tf_op jit(solution)/shard_map/ppermute | solution.py:29
  296.7 36.2 %collective-permute-start.140 = (bf16[144,1024]{1,0:T(8,128)(2,1)}, bf16[144,1024]{1,0:T(8,128)(2,1)}, u32[]{:S(2)}, u32[]{:S(2)}) collective-permute-start(bf16[144,1024]{1,0:T(8,128)(2,1)} %add_convert_fusion.8), channel_id=1, source_target_pairs={{0,2},{1,3},{2,0},{3,1},{4,6},{5,7},{6,4},{7,5},{8,10},{9,11},{10,... | collective-permute-start | bytes 884744 | tf_op jit(solution)/shard_map/ppermute | solution.py:29
  300.2 33.8 %collective-permute-start.142 = (bf16[144,1024]{1,0:T(8,128)(2,1)}, bf16[144,1024]{1,0:T(8,128)(2,1)}, u32[]{:S(2)}, u32[]{:S(2)}) collective-permute-start(bf16[144,1024]{1,0:T(8,128)(2,1)} %add_convert_fusion.7), channel_id=1, source_target_pairs={{0,4},{1,5},{2,6},{3,7},{4,0},{5,1},{6,2},{7,3},{8,12},{9,13},{10,... | collective-permute-start | bytes 884744 | tf_op jit(solution)/shard_map/ppermute | solution.py:29
  302.3 32.8 %collective-permute-start.144 = (bf16[144,1024]{1,0:T(8,128)(2,1)}, bf16[144,1024]{1,0:T(8,128)(2,1)}, u32[]{:S(2)}, u32[]{:S(2)}) collective-permute-start(bf16[144,1024]{1,0:T(8,128)(2,1)} %add_convert_fusion.6), channel_id=1, source_target_pairs={{0,6},{1,7},{2,4},{3,5},{4,2},{5,3},{6,0},{7,1},{8,14},{9,15},{10,... | collective-permute-start | bytes 884744 | tf_op jit(solution)/shard_map/ppermute | solution.py:29
  373.7 139.6 %collective-permute-start.146 = (bf16[16,768]{1,0:T(8,128)(2,1)}, bf16[16,768]{1,0:T(8,128)(2,1)}, u32[]{:S(2)}, u32[]{:S(2)}) collective-permute-start(bf16[16,768]{1,0:T(8,128)(2,1)} %pad_maximum_fusion.11), channel_id=1, source_target_pairs={{0,16},{1,17},{2,18},{3,19},{4,20},{5,21},{6,22},{7,23},{8,24},{9,... | collective-permute-start | bytes 73736 | tf_op jit(solution)/shard_map/ppermute | solution.py:29
  423.2 49.2 %collective-permute-start.128 = (bf16[144,1024]{1,0:T(8,128)(2,1)}, bf16[144,1024]{1,0:T(8,128)(2,1)}, u32[]{:S(2)}, u32[]{:S(2)}) collective-permute-start(bf16[144,1024]{1,0:T(8,128)(2,1)} %get-tuple-element.257), channel_id=1, source_target_pairs={{0,1},{1,0},{2,3},{3,2},{4,5},{5,4},{6,7},{7,6},{8,9},{9,8},{10,11... | collective-permute-start | bytes 884744 | tf_op jit(solution)/shard_map/ppermute | solution.py:29
  440.3 32.1 %collective-permute-start.130 = (bf16[144,1024]{1,0:T(8,128)(2,1)}, bf16[144,1024]{1,0:T(8,128)(2,1)}, u32[]{:S(2)}, u32[]{:S(2)}) collective-permute-start(bf16[144,1024]{1,0:T(8,128)(2,1)} %add_convert_fusion.11), channel_id=1, source_target_pairs={{0,2},{1,3},{2,0},{3,1},{4,6},{5,7},{6,4},{7,5},{8,10},{9,11},{10,... | collective-permute-start | bytes 884744 | tf_op jit(solution)/shard_map/ppermute | solution.py:29
  442.3 31.3 %collective-permute-start.132 = (bf16[144,1024]{1,0:T(8,128)(2,1)}, bf16[144,1024]{1,0:T(8,128)(2,1)}, u32[]{:S(2)}, u32[]{:S(2)}) collective-permute-start(bf16[144,1024]{1,0:T(8,128)(2,1)} %add_convert_fusion.10), channel_id=1, source_target_pairs={{0,4},{1,5},{2,6},{3,7},{4,0},{5,1},{6,2},{7,3},{8,12},{9,13},{10,... | collective-permute-start | bytes 884744 | tf_op jit(solution)/shard_map/ppermute | solution.py:29
  443.9 30.6 %collective-permute-start.134 = (bf16[144,1024]{1,0:T(8,128)(2,1)}, bf16[144,1024]{1,0:T(8,128)(2,1)}, u32[]{:S(2)}, u32[]{:S(2)}) collective-permute-start(bf16[144,1024]{1,0:T(8,128)(2,1)} %add_convert_fusion.9), channel_id=1, source_target_pairs={{0,6},{1,7},{2,4},{3,5},{4,2},{5,3},{6,0},{7,1},{8,14},{9,15},{10,... | collective-permute-start | bytes 884744 | tf_op jit(solution)/shard_map/ppermute | solution.py:29
  (304 other events, 4170.8 us)
